TPU v7x, 32 devices: a whole 2x2x4 slice. The times are simulated.
32 devices in a mesh: narrow: 4 (over z), wide: 8 (over y, x, core).
Axes of the slice: x: 2, y: 2, z: 4, core: 2. Of those that a mesh axis runs over, the one named last changes fastest.
Arguments:
- pixels: int32 [12, 262144], P(None, ('narrow', 'wide')), may hold values from 0 to 255
- noise: float32 [12, 262144], P(None, ('narrow', 'wide')), may hold values from 0 to 1
- depth: int32 [1024], P(('narrow', 'wide')), may hold values from 5 to 8, as said below
- step_count: int32 [], replicated, may hold values from 2 to 20
- conv_in: float32 [2, 512, 54], P(None, 'wide'), may hold values from -0.4082483 to 0.4082483
- conv_mid: float32 [2, 512, 512], P(None, 'wide'), may hold values from -0.13258252 to 0.13258252
- conv_out: float32 [2, 108, 512], P(None, None, 'wide'), may hold values from -0.044194174 to 0.044194174
- hidden_bias: float32 [2, 2, 512], P(None, None, 'wide'), may hold values from -1.5 to 1.5
- flow_small: float32 [2, 12, 15], replicated, may hold values from -0.3 to 0.3
- prior_conv: float32 [12, 55], replicated, may hold values from -0.12 to 0.12
- mean_in: float32 [2, 512, 54], P(None, 'wide'), may hold values from -3.8146973e-06 to 3.8146973e-06
- mean_mid: float32 [2, 512, 512], P(None, 'wide'), may hold values from -6.67572e-06 to 6.67572e-06
- mean_out: float32 [2, 108, 512], P(None, None, 'wide'), may hold values from -7.6293945e-05 to 7.6293945e-05
- mean_bias: float32 [2, 2, 512], P(None, None, 'wide'), may hold values from -9.536743e-06 to 9.536743e-06
- mean_small: float32 [2, 12, 15], replicated, may hold values from -0.0625 to 0.0625
- mean_prior: float32 [12, 55], replicated, may hold values from -0.03125 to 0.03125
- square_in: float32 [2, 512, 54], P(None, 'wide'), may hold values from 1.953125e-14 to 3.125e-13
- square_mid: float32 [2, 512, 512], P(None, 'wide'), may hold values from 4.3945313e-14 to 7.03125e-13
- square_out: float32 [2, 108, 512], P(None, None, 'wide'), may hold values from 7.8125e-12 to 1.25e-10
- square_bias: float32 [2, 2, 512], P(None, None, 'wide'), may hold values from 1.2207031e-13 to 1.953125e-12
- square_small: float32 [2, 12, 15], replicated, may hold values from 5e-06 to 8e-05
- square_prior: float32 [12, 55], replicated, may hold values from 1.25e-06 to 2e-05
Outputs:
- loss: float32 [], replicated
- new_conv_in: float32 [2, 512, 54], P(None, 'wide')
- new_mean_in: float32 [2, 512, 54], P(None, 'wide')
- new_square_in: float32 [2, 512, 54], P(None, 'wide')
- new_conv_mid: float32 [2, 512, 512], P(None, 'wide')
- new_mean_mid: float32 [2, 512, 512], P(None, 'wide')
- new_square_mid: float32 [2, 512, 512], P(None, 'wide')
- new_conv_out: float32 [2, 108, 512], P(None, None, 'wide')
- new_mean_out: float32 [2, 108, 512], P(None, None, 'wide')
- new_square_out: float32 [2, 108, 512], P(None, None, 'wide')
- new_hidden_bias: float32 [2, 2, 512], P(None, None, 'wide')
- new_mean_bias: float32 [2, 2, 512], P(None, None, 'wide')
- new_square_bias: float32 [2, 2, 512], P(None, None, 'wide')
- new_flow_small: float32 [2, 12, 15], replicated
- new_mean_small: float32 [2, 12, 15], replicated
- new_square_small: float32 [2, 12, 15], replicated
- new_prior_conv: float32 [12, 55], replicated
- new_mean_prior: float32 [12, 55], replicated
- new_square_prior: float32 [12, 55], replicated
Inputs may be any that keep to these rules, and one draw needn't show every extreme that they name: `depth`: each entry is 5 or 8; the share of 5 rises with the image index from about a tenth to about nine tenths; the first image has 8, the last 5.
All inputs are finite; a program needn't handle non-finite values.
Results may differ from a plain program's by a relative error of at most 0.00085.
The roundings to bfloat16 on the way count: a program that leaves them out, or rounds other values in their place, can miss the bound.
Values may be sent and summed in bfloat16 or wider, within the bound.
A program may use at most 192 MiB of HBM per device.

v0:
```python
import math

import jax
import jax.numpy as jnp
from jax import lax
from jax.sharding import PartitionSpec as P

highest = lax.Precision.HIGHEST
learn_rate = 0.02
beta_one = 0.9
beta_two = 0.999
epsilon = 1e-08
decay_rate = 0.01
penalty_weight = 0.5
tap_offsets = [(row_step, col_step) for row_step in (-1, 0, 1) for col_step in (-1, 0, 1)]
contract_last = (((1,), (1,)), ((), ()))
contract_first = (((0,), (0,)), ((), ()))


def tap_mask(count, row_step, col_step):
    index = jnp.arange(count, dtype=jnp.int32)
    row = index // 16 % 16
    column = index % 16
    return (
        (row + row_step >= 0)
        & (row + row_step < 16)
        & (column + col_step >= 0)
        & (column + col_step < 16)
    )


def shifted(values, row_step, col_step):
    moved = jnp.roll(values, -(16 * row_step + col_step), axis=1)
    return jnp.where(
        tap_mask(values.shape[1], row_step, col_step)[None, :], moved, jnp.zeros_like(moved)
    )


def shifted_back(values, row_step, col_step):
    masked = jnp.where(
        tap_mask(values.shape[1], row_step, col_step)[None, :], values, jnp.zeros_like(values)
    )
    return jnp.roll(masked, 16 * row_step + col_step, axis=1)


def all_taps(values):
    return jnp.concatenate(
        [shifted(values, row_step, col_step) for row_step, col_step in tap_offsets], axis=0
    )


def fold_taps(values, width):
    total = shifted_back(values[0:width], tap_offsets[0][0], tap_offsets[0][1])
    for index in range(1, 9):
        total = total + shifted_back(
            values[width * index : width * index + width],
            tap_offsets[index][0],
            tap_offsets[index][1],
        )
    return total


def dequantize(pixels, noise, depth):
    coarse = jnp.repeat(depth, 256) == 5
    divisor = jnp.where(coarse, 8, 1).astype(jnp.int32)
    levels = jnp.where(coarse, 32.0, 256.0).astype(jnp.float32)
    quant = (pixels // divisor[None, :]).astype(jnp.float32)
    return (quant + noise) / levels[None, :] - 0.5


def mixing_matrix(lu_part):
    lower = jnp.tril(lu_part, -1) + jnp.eye(12, dtype=lu_part.dtype)
    upper = jnp.triu(lu_part, 1) + jnp.diag(jnp.exp(jnp.diag(lu_part)))
    return jnp.dot(lower, upper, precision=highest)[::-1]


def prepare(state, small):
    lu_part = small[:, 0:12]
    moved = (state + small[:, 12:13]) * jnp.exp(small[:, 13:14])
    mixed = jnp.dot(mixing_matrix(lu_part), moved, precision=highest)
    logdet = state.shape[1] * (jnp.sum(small[:, 13]) + jnp.sum(jnp.diag(lu_part)))
    return (mixed, logdet)


def prior_logp(latent, prior):
    first = latent[0:6]
    rest = latent[6:12]
    stats = jnp.dot(prior[:, 0:54], all_taps(first), precision=highest) + prior[:, 54:55]
    centre = stats[0:6]
    log_sd = stats[6:12]
    gauss = -0.5 * first * first - 0.5 * jnp.square((rest - centre) * jnp.exp(-log_sd)) - log_sd
    return jnp.sum(gauss) - latent.shape[1] * 6.0 * math.log(2.0 * math.pi)


def fetch_forward(sent, layer):
    return (
        lax.all_gather(sent[0][layer], "wide", axis=0, tiled=True),
        lax.all_gather(sent[1][layer], "wide", axis=0, tiled=True),
        lax.all_gather(sent[2][layer], "wide", axis=1, tiled=True),
        lax.all_gather(sent[3][layer], "wide", axis=1, tiled=True),
    )


def fetch_backward(sent, layer):
    return (
        lax.all_gather(sent[0][layer], "wide", axis=0, tiled=True),
        lax.all_gather(sent[1][layer], "wide", axis=0, tiled=True),
        lax.all_gather(sent[2][layer], "wide", axis=1, tiled=True),
        lax.all_gather(sent[3][layer], "wide", axis=1, tiled=True),
    )


def reduce_layer(grads):
    totals = lax.psum((grads[0], grads[1], grads[2], grads[3]), "narrow")
    return (
        lax.psum_scatter(totals[0], "wide", scatter_dimension=0, tiled=True),
        lax.psum_scatter(totals[1], "wide", scatter_dimension=0, tiled=True),
        lax.psum_scatter(totals[2], "wide", scatter_dimension=1, tiled=True),
        lax.psum_scatter(totals[3], "wide", scatter_dimension=1, tiled=True),
    )


def forward_layer(state, small, weights):
    w_first, w_second, w_third, biases = weights
    mixed, logdet = prepare(state, small)
    kept = mixed[0:6]
    other = mixed[6:12]
    stacked = all_taps(kept.astype(jnp.bfloat16))
    first = jnp.dot(w_first, stacked, preferred_element_type=jnp.float32) + biases[0][
        :, None
    ].astype(jnp.float32)
    hidden_one = jax.nn.relu(first).astype(jnp.bfloat16)
    second = jnp.dot(w_second, hidden_one, preferred_element_type=jnp.float32) + biases[1][
        :, None
    ].astype(jnp.float32)
    hidden_two = jax.nn.relu(second).astype(jnp.bfloat16)
    taps_out = jnp.dot(w_third, hidden_two, preferred_element_type=jnp.float32)
    summed = shifted(taps_out[0:12], tap_offsets[0][0], tap_offsets[0][1])
    for index in range(1, 9):
        summed = summed + shifted(
            taps_out[12 * index : 12 * index + 12], tap_offsets[index][0], tap_offsets[index][1]
        )
    output = summed + small[:, 14:15]
    scale = jax.nn.sigmoid(output[6:12] + 2.0)
    other_new = (other + output[0:6]) * scale
    logdet = logdet + jnp.sum(jnp.log(scale))
    result = jnp.concatenate([kept, other_new], axis=0)
    return (result, logdet, (stacked, hidden_one, hidden_two, other, output, scale))


def backward_layer(state, small, weights, cache, grad_result, coeff):
    w_first, w_second, w_third, biases = weights
    stacked, hidden_one, hidden_two, other, output, scale = cache
    grad_new = grad_result[6:12]
    grad_other = grad_new * scale
    grad_raw = (grad_new * (other + output[0:6]) * scale + coeff) * (1.0 - scale)
    grad_output = jnp.concatenate([grad_other, grad_raw], axis=0)
    grad_out_bias = jnp.sum(grad_output, axis=1)
    low_output = grad_output.astype(jnp.bfloat16)
    taps_back = jnp.concatenate(
        [shifted_back(low_output, row_step, col_step) for row_step, col_step in tap_offsets], axis=0
    )
    grad_third = lax.dot_general(
        taps_back, hidden_two, contract_last, preferred_element_type=jnp.float32
    )
    grad_two = lax.dot_general(
        w_third, taps_back, contract_first, preferred_element_type=jnp.float32
    )
    low_two = jnp.where(hidden_two > 0, grad_two, 0.0).astype(jnp.bfloat16)
    grad_second = lax.dot_general(
        low_two, hidden_one, contract_last, preferred_element_type=jnp.float32
    )
    grad_one = lax.dot_general(
        w_second, low_two, contract_first, preferred_element_type=jnp.float32
    )
    low_one = jnp.where(hidden_one > 0, grad_one, 0.0).astype(jnp.bfloat16)
    grad_first = lax.dot_general(
        low_one, stacked, contract_last, preferred_element_type=jnp.float32
    )
    grad_stacked = lax.dot_general(
        w_first, low_one, contract_first, preferred_element_type=jnp.float32
    )
    grad_biases = jnp.stack(
        [jnp.sum(low_one, axis=1, dtype=jnp.float32), jnp.sum(low_two, axis=1, dtype=jnp.float32)]
    )
    grad_kept = grad_result[0:6] + fold_taps(grad_stacked, 6)
    grad_mixed = jnp.concatenate([grad_kept, grad_other], axis=0)
    _, pullback = jax.vjp(prepare, state, small)
    grad_state, grad_small = pullback((grad_mixed, coeff))
    grad_small = grad_small.at[:, 14].add(grad_out_bias)
    return (grad_state, grad_small, (grad_first, grad_second, grad_third, grad_biases))


def adamw(weight, grad, first, second, step):
    first_new = beta_one * first + (1.0 - beta_one) * grad
    second_new = beta_two * second + (1.0 - beta_two) * grad * grad
    fix_one = 1.0 - jnp.power(beta_one, step)
    fix_two = 1.0 - jnp.power(beta_two, step)
    update = first_new / fix_one / (jnp.sqrt(second_new / fix_two) + epsilon) + decay_rate * weight
    return (weight - learn_rate * update, first_new, second_new)


def shards(
    pixels,
    noise,
    depth,
    step_count,
    conv_in,
    conv_mid,
    conv_out,
    hidden_bias,
    flow_small,
    prior_conv,
    mean_in,
    mean_mid,
    mean_out,
    mean_bias,
    mean_small,
    mean_prior,
    square_in,
    square_mid,
    square_out,
    square_bias,
    square_small,
    square_prior,
):
    layers = conv_in.shape[0]
    count = pixels.shape[1]
    total_pixels = count * lax.axis_size("narrow") * lax.axis_size("wide")
    coeff = jnp.float32(-1.0 / (total_pixels * 12 * math.log(2.0)))
    sent = (
        conv_in.astype(jnp.bfloat16),
        conv_mid.astype(jnp.bfloat16),
        conv_out.astype(jnp.bfloat16),
        hidden_bias.astype(jnp.bfloat16),
    )
    state = dequantize(pixels, noise, depth)
    inputs = []
    caches = []
    gathered = []
    logdet = jnp.zeros((), jnp.float32)
    for layer in range(layers):
        weights = fetch_forward(sent, layer)
        inputs.append(state)
        state, term, cache = forward_layer(state, flow_small[layer], weights)
        caches.append(cache)
        gathered.append(weights)
        logdet = logdet + term
    likely, prior_pull = jax.vjp(prior_logp, state, prior_conv)
    sums = lax.psum(
        (
            jnp.sum(state, axis=1),
            jnp.sum(state * state, axis=1),
            likely + logdet,
            jnp.sum(depth).astype(jnp.float32),
        ),
        ("narrow", "wide"),
    )
    mean = sums[0] / total_pixels
    var = sums[1] / total_pixels - mean * mean
    penalty = penalty_weight * jnp.sum(mean * mean + jnp.square(var - 1.0))
    loss = coeff * sums[2] + penalty + sums[3] / (total_pixels // 256)
    grad_first_sum = penalty_weight * (2.0 * mean - 4.0 * (var - 1.0) * mean) / total_pixels
    grad_square_sum = penalty_weight * 2.0 * (var - 1.0) / total_pixels
    grad_state, grad_prior = prior_pull(coeff)
    grad_state = grad_state + grad_first_sum[:, None] + 2.0 * state * grad_square_sum[:, None]
    small_grads = [None] * layers
    reduced = [None] * layers
    for layer in reversed(range(layers)):
        weights = fetch_backward(sent, layer)
        grad_state, grad_small, grads = backward_layer(
            inputs[layer], flow_small[layer], weights, caches[layer], grad_state, coeff
        )
        small_grads[layer] = grad_small
        reduced[layer] = reduce_layer(grads)
    small_total, prior_total = lax.psum((jnp.stack(small_grads), grad_prior), ("narrow", "wide"))
    step = step_count.astype(jnp.float32)
    params = (conv_in, conv_mid, conv_out, hidden_bias, flow_small, prior_conv)
    grads_all = tuple(
        (jnp.stack([reduced[layer][index] for layer in range(layers)]) for index in range(4))
    ) + (small_total, prior_total)
    firsts = (mean_in, mean_mid, mean_out, mean_bias, mean_small, mean_prior)
    seconds = (square_in, square_mid, square_out, square_bias, square_small, square_prior)
    results = [loss]
    for index in range(6):
        results.extend(adamw(params[index], grads_all[index], firsts[index], seconds[index], step))
    return tuple(results)


def solution(mesh):
    return jax.shard_map(
        shards,
        mesh=mesh,
        in_specs=(
            P(None, ("narrow", "wide")),
            P(None, ("narrow", "wide")),
            P(("narrow", "wide")),
            P(),
            P(None, "wide", None),
            P(None, "wide", None),
            P(None, None, "wide"),
            P(None, None, "wide"),
            P(),
            P(),
            P(None, "wide", None),
            P(None, "wide", None),
            P(None, None, "wide"),
            P(None, None, "wide"),
            P(),
            P(),
            P(None, "wide", None),
            P(None, "wide", None),
            P(None, None, "wide"),
            P(None, None, "wide"),
            P(),
            P(),
        ),
        out_specs=(
            P(),
            P(None, "wide", None),
            P(None, "wide", None),
            P(None, "wide", None),
            P(None, "wide", None),
            P(None, "wide", None),
            P(None, "wide", None),
            P(None, None, "wide"),
            P(None, None, "wide"),
            P(None, None, "wide"),
            P(None, None, "wide"),
            P(None, None, "wide"),
            P(None, None, "wide"),
            P(),
            P(),
            P(),
            P(),
            P(),
            P(),
        ),
        check_vma=False,
    )
```

profile of v0, /device:TPU:0, one launch (start us, length us, event | category | flops | bytes accessed | tf_op | source)
XLA Modules:
  0.0 755.4 jit_solution(8432352283440684452)
XLA Ops:
  12.8 6.5 fusion.7
  26.0 10.7 %all-gather.3 = bf16[1,108,512]{1,2,0:T(8,128)(2,1)S(1)} all-gather(bf16[1,108,64]{1,2,0:T(8,128)(2,1)S(1)} %get-tuple-element.339), channel_id=5, replica_groups=mesh['narrow'=4,'wide'=8] {'wide'}, dimensions={2}, use_global_device_ids=true | all-gather | bytes 124416 | tf_op jit(solution)/shard_map/all_gather | solution.py:99
  37.7 9.3 %all-gather = bf16[1,512,54]{2,0,1:T(2,128)(2,1)S(1)} all-gather(bf16[1,64,54]{2,0,1:T(2,128)(2,1)S(1)} %get-tuple-element.341), channel_id=2, replica_groups=mesh['narrow'=4,'wide'=8] {'wide'}, dimensions={1}, use_global_device_ids=true | all-gather | bytes 62208 | tf_op jit(solution)/shard_map/all_gather | solution.py:97
  47.8 8.7 %all-gather.1 = bf16[1,2,512]{1,0,2:T(2,128)(2,1)S(1)} all-gather(bf16[1,2,64]{1,0,2:T(2,128)(2,1)S(1)} %get-tuple-element.343), channel_id=3, replica_groups=mesh['narrow'=4,'wide'=8] {'wide'}, dimensions={2}, use_global_device_ids=true | all-gather | bytes 2304 | tf_op jit(solution)/shard_map/all_gather | solution.py:100
  56.5 2.8 fusion.79
  59.3 9.8 %all-gather.2 = bf16[1,512,512]{2,1,0:T(8,128)(2,1)S(1)} all-gather(bf16[1,64,512]{2,1,0:T(8,128)(2,1)S(1)} %get-tuple-element.305), channel_id=4, replica_groups=mesh['narrow'=4,'wide'=8] {'wide'}, dimensions={1}, use_global_device_ids=true | all-gather | bytes 589824 | tf_op jit(solution)/shard_map/all_gather | solution.py:98
  70.1 1.7 concatenate.326
  71.7 6.6 maximum_convert_fusion.3
  78.4 8.2 %maximum_convert_fusion.2 = bf16[8192,512]{1,0:T(8,128)(2,1)S(1)} fusion(bf16[8192,512]{1,0:T(8,128)(2,1)} %maximum_convert_fusion.3, f32[512]{0:T(512)S(1)} %get-tuple-element.155, bf16[1,512,512]{2,1,0:T(8,128)(2,1)S(1)} %all-gather.2), kind=kOutput, calls=%fused_computation.16 | convolution fusion | flops 4307550208 | bytes 17303552 | tf_op jit(solution)/shard_map/dot_general | solution.py:133
  86.6 2.8 convolution_bitcast_fusion.1
  90.6 1.5 fusion.195
  95.9 2.5 fusion.19
  110.2 18.6 %all-gather.7 = bf16[1,108,512]{1,2,0:T(8,128)(2,1)S(1)} all-gather(bf16[1,108,64]{1,2,0:T(8,128)(2,1)S(1)} %copy-done.60), channel_id=9, replica_groups=mesh['narrow'=4,'wide'=8] {'wide'}, dimensions={2}, use_global_device_ids=true | all-gather | bytes 124416 | tf_op jit(solution)/shard_map/all_gather | solution.py:99
  128.9 9.3 %all-gather.4 = bf16[1,512,54]{2,0,1:T(2,128)(2,1)S(1)} all-gather(bf16[1,64,54]{2,0,1:T(2,128)(2,1)S(1)} %copy-done.52), channel_id=6, replica_groups=mesh['narrow'=4,'wide'=8] {'wide'}, dimensions={1}, use_global_device_ids=true | all-gather | bytes 62208 | tf_op jit(solution)/shard_map/all_gather | solution.py:97
  138.3 8.3 %all-gather.5 = bf16[1,2,512]{1,0,2:T(2,128)(2,1)S(1)} all-gather(bf16[1,2,64]{1,0,2:T(2,128)(2,1)S(1)} %copy-done.51), channel_id=7, replica_groups=mesh['narrow'=4,'wide'=8] {'wide'}, dimensions={2}, use_global_device_ids=true | all-gather | bytes 2304 | tf_op jit(solution)/shard_map/all_gather | solution.py:100
  146.6 2.8 fusion.73
  149.4 10.8 %all-gather.6 = bf16[1,512,512]{2,1,0:T(8,128)(2,1)} all-gather(bf16[1,64,512]{2,1,0:T(8,128)(2,1)S(1)} %get-tuple-element.304), channel_id=8, replica_groups=mesh['narrow'=4,'wide'=8] {'wide'}, dimensions={1}, use_global_device_ids=true | all-gather | bytes 589824 | tf_op jit(solution)/shard_map/all_gather | solution.py:98
  165.4 1.7 maximum_select_fusion.34
  167.1 1.7 maximum_select_fusion.36
  168.7 1.7 maximum_select_fusion.35
  170.4 17.5 %concatenate.344 = bf16[54,8192]{1,0:T(8,128)(2,1)} concatenate(bf16[6,8192]{1,0:T(8,128)(2,1)S(1)} %maximum_select_fusion.32, bf16[6,8192]{1,0:T(8,128)(2,1)S(1)} %maximum_select_fusion.33, bf16[6,8192]{1,0:T(8,128)(2,1)} %maximum_select_fusion.34, bf16[6,8192]{1,0:T(8,128)(2,1)} %maximum_select_fusion.35, bf16[6,8192]{1,0:T(8,128)(2,1)S(1)} %get-tuple-element.201, ...), dimensions={0} | concatenate | bytes 1769472 | tf_op jit(solution)/shard_map/concatenate | solution.py:47
  187.9 7.0 maximum_convert_fusion.1
  195.0 8.2 %maximum_convert_fusion = bf16[8192,512]{1,0:T(8,128)(2,1)S(1)} fusion(bf16[8192,512]{1,0:T(8,128)(2,1)} %maximum_convert_fusion.1, f32[512]{0:T(512)S(1)} %get-tuple-element.153, bf16[1,512,512]{2,1,0:T(8,128)(2,1)S(1)} %copy-done.42), kind=kOutput, calls=%fused_computation.14 | convolution fusion | flops 4307550208 | bytes 17303552 | tf_op jit(solution)/shard_map/dot_general | solution.py:133
  203.2 2.8 convolution_bitcast_fusion
  218.7 10.9 %concatenate.361 = f32[54,8192]{1,0:T(8,128)S(1)} concatenate(f32[6,8192]{1,0:T(8,128)} %maximum_select_fusion.16, f32[6,8192]{1,0:T(8,128)} %maximum_select_fusion.17, f32[6,8192]{1,0:T(8,128)} %maximum_select_fusion.18, f32[6,8192]{1,0:T(8,128)} %maximum_select_fusion.19, f32[6,8192]{1,0:T(8,128)S(1)} %broadcast_select_fusion.18, f32[6,8192]{1,0:T(8,128)} %maximum_select_fusion.20, ...), dimensions={0} | concatenate | bytes 3538944 | tf_op jit(solution)/shard_map/jvp()/concatenate | solution.py:47
  229.6 1.9 fusion
  231.4 3.1 fusion.13
  234.8 1.5 fusion.182
  237.0 1.6 convolution_bitcast_fusion.2
  244.7 39.5 %all-reduce.31 = (f32[12]{0:T(128)S(1)}, f32[12]{0:T(128)S(1)}) all-reduce(f32[12]{0:T(128)S(1)} %get-tuple-element.152, f32[12]{0:T(128)S(1)} %get-tuple-element.151), channel_id=1, replica_groups=mesh['narrow'=4,'wide'=8] {'narrow','wide'}, use_global_device_ids=true, to_apply=%region_11.12 | all-reduce | flops 24 | bytes 192 | tf_op jit(solution)/shard_map/psum | solution.py:250
  287.9 1.9 fusion.68
  298.5 22.0 %concatenate.372 = bf16[108,8192]{1,0:T(8,128)(2,1)} concatenate(bf16[12,8192]{1,0:T(8,128)(2,1)} %pad_maximum_fusion.9, bf16[12,8192]{1,0:T(8,128)(2,1)} %pad_maximum_fusion.10, bf16[12,8192]{1,0:T(8,128)(2,1)} %pad_maximum_fusion.11, bf16[12,8192]{1,0:T(8,128)(2,1)} %pad_maximum_fusion.12, bf16[12,8192]{1,0:T(8,128)(2,1)S(1)} %get-tuple-element.299, ...), dimensions={0} | concatenate | bytes 3538944 | tf_op jit(solution)/shard_map/concatenate | solution.py:160
  320.5 10.4 %convert_reduce_fusion = (f32[512]{0:T(512)S(1)}, bf16[8192,512]{1,0:T(8,128)(2,1)}) fusion(bf16[108,8192]{1,0:T(8,128)(2,1)} %concatenate.372, bf16[1,108,512]{1,2,0:T(8,128)(2,1)} %copy-done.39, bf16[8192,512]{1,0:T(8,128)(2,1)} %copy-done.1), kind=kOutput, calls=%fused_computation.6 | convolution fusion | flops 926940672 | bytes 18659328 | tf_op jit(solution)/shard_map/dot_general | solution.py:166
  330.8 11.4 %convert_reduce_fusion.1 = (f32[512]{0:T(512)S(1)}, bf16[8192,512]{1,0:T(8,128)(2,1)}) fusion(bf16[8192,512]{1,0:T(8,128)(2,1)} %get-tuple-element.371, bf16[1,512,512]{2,1,0:T(8,128)(2,1)S(1)} %copy-done.43, bf16[8192,512]{1,0:T(8,128)(2,1)} %maximum_convert_fusion.1), kind=kOutput, calls=%fused_computation.7 | convolution fusion | flops 4315938304 | bytes 25692160 | tf_op jit(solution)/shard_map/dot_general | solution.py:173
  343.5 6.1 convolution_bitcast_fusion.4
  361.3 24.5 %concatenate.391 = bf16[108,8192]{1,0:T(8,128)(2,1)} concatenate(bf16[12,8192]{1,0:T(8,128)(2,1)} %pad_maximum_fusion.17, bf16[12,8192]{1,0:T(8,128)(2,1)} %pad_maximum_fusion.18, bf16[12,8192]{1,0:T(8,128)(2,1)} %pad_maximum_fusion.19, bf16[12,8192]{1,0:T(8,128)(2,1)S(1)} %pad_maximum_fusion.20, bf16[12,8192]{1,0:T(8,128)(2,1)} %get-tuple-element.291, ...), dimensions={0} | concatenate | bytes 3538944 | tf_op jit(solution)/shard_map/concatenate | solution.py:160
  385.8 8.6 %convert_reduce_fusion.2 = (f32[512]{0:T(512)S(1)}, bf16[8192,512]{1,0:T(8,128)(2,1)}) fusion(bf16[108,8192]{1,0:T(8,128)(2,1)} %concatenate.391, bf16[1,108,512]{1,2,0:T(8,128)(2,1)S(1)} %copy-done.38, bf16[8192,512]{1,0:T(8,128)(2,1)} %copy-done), kind=kOutput, calls=%fused_computation.8 | convolution fusion | flops 926940672 | bytes 18659328 | tf_op jit(solution)/shard_map/dot_general | solution.py:166
  394.4 11.5 %convert_reduce_fusion.3 = (f32[512]{0:T(512)S(1)}, bf16[8192,512]{1,0:T(8,128)(2,1)}) fusion(bf16[8192,512]{1,0:T(8,128)(2,1)} %get-tuple-element.375, bf16[1,512,512]{2,1,0:T(8,128)(2,1)S(1)} %copy-done.41, bf16[8192,512]{1,0:T(8,128)(2,1)} %maximum_convert_fusion.3), kind=kOutput, calls=%fused_computation.9 | convolution fusion | flops 4315938304 | bytes 25692160 | tf_op jit(solution)/shard_map/dot_general | solution.py:173
  407.1 6.6 fusion.230
  413.8 6.7 fusion.229
  420.5 8.0 %fusion.234 = f32[108,512]{0,1:T(8,128)} fusion(bf16[108,8192]{1,0:T(8,128)(2,1)} %concatenate.372, bf16[8192,512]{1,0:T(8,128)(2,1)} %copy-done.1), kind=kOutput, calls=%fused_computation.484 | convolution fusion | flops 905969664 | bytes 10379264 | tf_op jit(solution)/shard_map/dot_general | solution.py:163
  428.6 8.0 %fusion.233 = f32[108,512]{0,1:T(8,128)} fusion(bf16[108,8192]{1,0:T(8,128)(2,1)} %concatenate.391, bf16[8192,512]{1,0:T(8,128)(2,1)} %copy-done), kind=kOutput, calls=%fused_computation.483 | convolution fusion | flops 905969664 | bytes 10379264 | tf_op jit(solution)/shard_map/dot_general | solution.py:163
  436.8 1.4 copy.151
  438.2 2.4 reduce-scatter.29.cloned.1.call-done
  440.5 1.4 copy.149
  441.9 35.8 %reduce-scatter.27.cloned.1.call-done = f32[64,54]{1,0:T(8,128)} async-done(((f32[512,54]{1,0:T(8,128)}), f32[64,54]{1,0:T(8,128)}) %reduce-scatter.27.cloned.1.call-update) | async-done | bytes 13840
  477.8 1.5 copy.147
  479.2 36.0 %reduce-scatter.25.cloned.1.call-done = f32[64,54]{1,0:T(8,128)} async-done(((f32[512,54]{1,0:T(8,128)}), f32[64,54]{1,0:T(8,128)}) %reduce-scatter.25.cloned.1.call-update) | async-done | bytes 13840
  515.2 1.5 copy.145
  516.6 35.6 %reduce-scatter.23.cloned.1.call-done = f32[108,64]{0,1:T(8,128)} async-done(((f32[108,512]{0,1:T(8,128)}), f32[108,64]{0,1:T(8,128)}) %reduce-scatter.23.cloned.1.call-update) | async-done | bytes 27664 | tf_op jit(solution)/shard_map/reduce_scatter | solution.py:118
  552.2 36.8 %reduce-scatter.21.cloned.1.call-done = f32[108,64]{0,1:T(8,128)} async-done(((f32[108,512]{0,1:T(8,128)}), f32[108,64]{0,1:T(8,128)}) %reduce-scatter.21.cloned.1.call-update) | async-done | bytes 27664 | tf_op jit(solution)/shard_map/reduce_scatter | solution.py:118
  589.5 11.3 %fusion.232 = f32[512,512]{1,0:T(8,128)} fusion(bf16[8192,512]{1,0:T(8,128)(2,1)} %get-tuple-element.371, bf16[8192,512]{1,0:T(8,128)(2,1)} %maximum_convert_fusion.1), kind=kOutput, calls=%fused_computation.482 | convolution fusion | flops 4294967296 | bytes 17825792 | tf_op jit(solution)/shard_map/dot_general | solution.py:170
  600.9 11.3 %fusion.231 = f32[512,512]{1,0:T(8,128)} fusion(bf16[8192,512]{1,0:T(8,128)(2,1)} %get-tuple-element.375, bf16[8192,512]{1,0:T(8,128)(2,1)} %maximum_convert_fusion.3), kind=kOutput, calls=%fused_computation.481 | convolution fusion | flops 4294967296 | bytes 17825792 | tf_op jit(solution)/shard_map/dot_general | solution.py:170
  613.1 2.6 fusion.31
  615.6 1.7 fusion.40
  617.3 6.1 convolution_bitcast_fusion.3
  636.5 2.2 scatter_fusion
  638.8 2.2 scatter_fusion.1
  644.9 1.5 fusion.45
  646.6 40.0 %all-reduce.30 = (f32[]{:T(128)}, f32[]{:T(128)}, f32[2,12,15]{1,2,0:T(8,128)S(1)}, f32[12,55]{1,0:T(8,128)S(1)}) all-reduce(f32[]{:T(128)S(6)} %add.1887, f32[]{:T(128)S(6)} %convert_element_type.145, f32[2,12,15]{1,2,0:T(8,128)S(1)} %pad_maximum_fusion.28, ...), channel_id=1, replica_groups=mesh['narrow'=4,'wide'=8] {'narrow','wide'}, use_global_device_ids=true, to_apply=%region_7.8 | all-reduce | flops 1022 | bytes 8176 | tf_op jit(solution)/shard_map/psum | solution.py:250
  695.3 11.9 %reduce-scatter.17.cloned.1.call-done = f32[64,512]{1,0:T(8,128)} async-done(((f32[512,512]{1,0:T(8,128)}), f32[64,512]{1,0:T(8,128)}) %reduce-scatter.17.cloned.1.call-update) | async-done | bytes 131088 | tf_op jit(solution)/shard_map/reduce_scatter | solution.py:117
  710.5 1.5 multiply_subtract_fusion.1
  711.9 33.1 %all-reduce.39.cloned.1.call-done = (f32[64,512]{1,0:T(8,128)}, f32[64,512]{1,0:T(8,128)}) async-done(((f32[64,512]{1,0:T(8,128)}, f32[64,512]{1,0:T(8,128)}), (f32[64,512]{1,0:T(8,128)}, f32[64,512]{1,0:T(8,128)})) %all-reduce.39.cloned.1.call-update) | async-done | bytes 262160 | tf_op jit(solution)/shard_map/psum | solution.py:114
  745.0 2.2 multiply_subtract_fusion
  (436 shorter events, 105.4 us)
Async XLA Ops:
  7.2 429.6 %reduce-scatter.31.cloned.1.call-start = ((), (), s32[]{:S(2)}) async-start(), calls=%async_computation.15 | async-start | bytes 294912
  10.2 68.2 %copy-start.2 = (f32[12,15]{0,1:T(8,128)}, f32[12,15]{0,1:T(8,128)S(1)}, u32[]{:S(2)}) copy-start(f32[12,15]{0,1:T(8,128)S(1)} %get-tuple-element.344) | copy-start | bytes 2164
  10.7 10.3 %copy-start.70 = (f32[12]{0:T(128)}, f32[12]{0:T(128)S(1)}, u32[]{:S(2)}) copy-start(f32[12]{0:T(128)S(1)} %get-tuple-element.354) | copy-start | bytes 148
  12.2 8.8 %copy-start.54 = (f32[12,12]{1,0:T(8,128)}, f32[12,12]{1,0:T(8,128)S(1)}, u32[]{:S(2)}) copy-start(f32[12,12]{1,0:T(8,128)S(1)} %rev.19) | copy-start | bytes 1732
  20.7 77.7 %copy-start.16 = (f32[12,8192]{1,0:T(8,128)}, f32[12,8192]{1,0:T(8,128)S(1)}, u32[]{:S(2)}) copy-start(f32[12,8192]{1,0:T(8,128)S(1)} %fusion.37) | copy-start | bytes 1179652
  36.7 49.9 %copy-start.37 = (bf16[1,108,512]{1,2,0:T(8,128)(2,1)}, bf16[1,108,512]{1,2,0:T(8,128)(2,1)S(1)}, u32[]{:S(2)}) copy-start(bf16[1,108,512]{1,2,0:T(8,128)(2,1)S(1)} %all-gather.3) | copy-start | bytes 331780
  69.1 9.3 %copy-start.40 = (bf16[1,512,512]{2,1,0:T(8,128)(2,1)}, bf16[1,512,512]{2,1,0:T(8,128)(2,1)S(1)}, u32[]{:S(2)}) copy-start(bf16[1,512,512]{2,1,0:T(8,128)(2,1)S(1)} %all-gather.2) | copy-start | bytes 1572868
  93.3 17.0 %copy-start.60 = (bf16[1,108,64]{1,2,0:T(8,128)(2,1)S(1)}, bf16[1,108,64]{1,2,0:T(8,128)(2,1)}, u32[]{:S(2)}) copy-start(bf16[1,108,64]{1,2,0:T(8,128)(2,1)} %get-tuple-element.338) | copy-start | bytes 41476
  93.3 35.6 %copy-start.52 = (bf16[1,64,54]{2,0,1:T(2,128)(2,1)S(1)}, bf16[1,64,54]{2,0,1:T(2,128)(2,1)}, u32[]{:S(2)}) copy-start(bf16[1,64,54]{2,0,1:T(2,128)(2,1)} %get-tuple-element.340) | copy-start | bytes 20740
  93.3 45.0 %copy-start.51 = (bf16[1,2,64]{1,0,2:T(2,128)(2,1)S(1)}, bf16[1,2,64]{1,0,2:T(2,128)(2,1)}, u32[]{:S(2)}) copy-start(bf16[1,2,64]{1,0,2:T(2,128)(2,1)} %get-tuple-element.342) | copy-start | bytes 772
  93.9 16.4 %copy-start.75 = (f32[12]{0:T(128)}, f32[12]{0:T(128)S(1)}, u32[]{:S(2)}) copy-start(f32[12]{0:T(128)S(1)} %get-tuple-element.351) | copy-start | bytes 148
  93.9 16.4 %copy-start.77 = (f32[12]{0:T(128)}, f32[12]{0:T(128)S(1)}, u32[]{:S(2)}) copy-start(f32[12]{0:T(128)S(1)} %get-tuple-element.352) | copy-start | bytes 148
  95.9 14.4 %copy-start.56 = (f32[12,12]{1,0:T(8,128)}, f32[12,12]{1,0:T(8,128)S(1)}, u32[]{:S(2)}) copy-start(f32[12,12]{1,0:T(8,128)S(1)} %rev.18) | copy-start | bytes 1732
  98.5 39.8 %copy-start.18 = (f32[6,8192]{1,0:T(8,128)}, f32[6,8192]{1,0:T(8,128)S(1)}, u32[]{:S(2)}) copy-start(f32[6,8192]{1,0:T(8,128)S(1)} %get-tuple-element.286) | copy-start | bytes 589828
  98.5 96.5 %copy-start.20 = (f32[6,8192]{1,0:T(8,128)}, f32[6,8192]{1,0:T(8,128)S(1)}, u32[]{:S(2)}) copy-start(f32[6,8192]{1,0:T(8,128)S(1)} %get-tuple-element.287) | copy-start | bytes 589828
  128.8 74.3 %copy-start.39 = (bf16[1,108,512]{1,2,0:T(8,128)(2,1)}, bf16[1,108,512]{1,2,0:T(8,128)(2,1)S(1)}, u32[]{:S(2)}) copy-start(bf16[1,108,512]{1,2,0:T(8,128)(2,1)S(1)} %all-gather.7) | copy-start | bytes 331780
  138.3 56.7 %copy-start.46 = (bf16[1,512,54]{1,2,0:T(8,128)(2,1)}, bf16[1,512,54]{1,2,0:T(8,128)(2,1)S(1)}, u32[]{:S(2)}) copy-start(bf16[1,512,54]{1,2,0:T(8,128)(2,1)S(1)} %copy.120) | copy-start | bytes 165892
  187.9 7.0 copy-start.42
  206.5 7.2 copy-start.33
  206.5 7.2 copy-start.67
  206.5 8.0 %copy-start.32 = (f32[6,8191]{1,0:T(8,128)S(1)}, f32[6,8191]{1,0:T(8,128)}, u32[]{:S(2)}) copy-start(f32[6,8191]{1,0:T(8,128)} %get-tuple-element.283) | copy-start | bytes 589756
  206.5 8.0 %copy-start.66 = (f32[6,1]{1,0:T(8,128)S(1)}, f32[6,1]{1,0:T(8,128)}, u32[]{:S(2)}) copy-start(f32[6,1]{1,0:T(8,128)} %get-tuple-element.285) | copy-start | bytes 76
  206.5 8.9 %copy-start.31 = (f32[6,8175]{1,0:T(8,128)S(1)}, f32[6,8175]{1,0:T(8,128)}, u32[]{:S(2)}) copy-start(f32[6,8175]{1,0:T(8,128)} %get-tuple-element.270) | copy-start | bytes 588604
  206.5 8.9 %copy-start.65 = (f32[6,17]{1,0:T(8,128)S(1)}, f32[6,17]{1,0:T(8,128)}, u32[]{:S(2)}) copy-start(f32[6,17]{1,0:T(8,128)} %get-tuple-element.272) | copy-start | bytes 1228
  206.5 9.7 %copy-start.64 = (f32[6,17]{1,0:T(8,128)S(1)}, f32[6,17]{1,0:T(8,128)}, u32[]{:S(2)}) copy-start(f32[6,17]{1,0:T(8,128)} %get-tuple-element.273) | copy-start | bytes 1228
  206.5 10.5 %copy-start.63 = (f32[6,16]{1,0:T(8,128)S(1)}, f32[6,16]{1,0:T(8,128)}, u32[]{:S(2)}) copy-start(f32[6,16]{1,0:T(8,128)} %get-tuple-element.276) | copy-start | bytes 1156
  206.5 11.3 %copy-start.62 = (f32[6,16]{1,0:T(8,128)S(1)}, f32[6,16]{1,0:T(8,128)}, u32[]{:S(2)}) copy-start(f32[6,16]{1,0:T(8,128)} %get-tuple-element.277) | copy-start | bytes 1156
  234.8 9.7 %copy-start.13 = (f32[6,8192]{1,0:T(8,128)}, f32[6,8192]{1,0:T(8,128)S(1)}, u32[]{:S(2)}) copy-start(f32[6,8192]{1,0:T(8,128)S(1)} %get-tuple-element.198) | copy-start | bytes 589828
  236.3 8.5 %copy-start.25 = (f32[6,8192]{1,0:T(8,128)}, f32[6,8192]{1,0:T(8,128)S(1)}, u32[]{:S(2)}) copy-start(f32[6,8192]{1,0:T(8,128)S(1)} %get-tuple-element.266) | copy-start | bytes 589828
  320.5 10.4 %copy-start.43 = (bf16[1,512,512]{2,1,0:T(8,128)(2,1)S(1)}, bf16[1,512,512]{2,1,0:T(8,128)(2,1)}, u32[]{:S(2)}) copy-start(bf16[1,512,512]{2,1,0:T(8,128)(2,1)} %all-gather.6) | copy-start | bytes 1572868
  330.8 12.6 %copy-start.47 = (bf16[1,512,54]{1,2,0:T(8,128)(2,1)S(1)}, bf16[1,512,54]{1,2,0:T(8,128)(2,1)}, u32[]{:S(2)}) copy-start(bf16[1,512,54]{1,2,0:T(8,128)(2,1)} %copy-done.46) | copy-start | bytes 165892
  343.2 97.3 %reduce-scatter.29.cloned.1.call-start = ((), (), s32[]{:S(2)}) async-start(), calls=%async_computation.14 | async-start | bytes 294912
  343.4 7.4 copy-start.29
  343.4 7.8 %copy-start.15 = (f32[6,8192]{1,0:T(8,128)S(1)}, f32[6,8192]{1,0:T(8,128)}, u32[]{:S(2)}) copy-start(f32[6,8192]{1,0:T(8,128)} %copy-done.14) | copy-start | bytes 589828
  343.4 7.8 %copy-start.19 = (f32[6,8192]{1,0:T(8,128)S(1)}, f32[6,8192]{1,0:T(8,128)}, u32[]{:S(2)}) copy-start(f32[6,8192]{1,0:T(8,128)} %copy-done.18) | copy-start | bytes 589828
  343.4 7.8 %copy-start.21 = (f32[6,8192]{1,0:T(8,128)S(1)}, f32[6,8192]{1,0:T(8,128)}, u32[]{:S(2)}) copy-start(f32[6,8192]{1,0:T(8,128)} %copy-done.20) | copy-start | bytes 589828
  343.5 7.8 %copy-start.57 = (f32[12,12]{1,0:T(8,128)S(1)}, f32[12,12]{1,0:T(8,128)}, u32[]{:S(2)}) copy-start(f32[12,12]{1,0:T(8,128)} %copy-done.56) | copy-start | bytes 1732
  343.5 7.8 %copy-start.76 = (f32[12]{0:T(128)S(1)}, f32[12]{0:T(128)}, u32[]{:S(2)}) copy-start(f32[12]{0:T(128)} %copy-done.75) | copy-start | bytes 148
  343.5 7.8 %copy-start.78 = (f32[12]{0:T(128)S(1)}, f32[12]{0:T(128)}, u32[]{:S(2)}) copy-start(f32[12]{0:T(128)} %copy-done.77) | copy-start | bytes 148
  351.2 34.6 %copy-start.38 = (bf16[1,108,512]{1,2,0:T(8,128)(2,1)S(1)}, bf16[1,108,512]{1,2,0:T(8,128)(2,1)}, u32[]{:S(2)}) copy-start(bf16[1,108,512]{1,2,0:T(8,128)(2,1)} %copy-done.37) | copy-start | bytes 331780
  385.8 8.6 %copy-start.41 = (bf16[1,512,512]{2,1,0:T(8,128)(2,1)S(1)}, bf16[1,512,512]{2,1,0:T(8,128)(2,1)}, u32[]{:S(2)}) copy-start(bf16[1,512,512]{2,1,0:T(8,128)(2,1)} %copy-done.40) | copy-start | bytes 1572868
  406.8 71.0 %reduce-scatter.27.cloned.1.call-start = ((), (), s32[]{:S(2)}) async-start(), calls=%async_computation.13 | async-start | bytes 294912
  413.7 101.5 %reduce-scatter.25.cloned.1.call-start = ((), (), s32[]{:S(2)}) async-start(), calls=%async_computation.12 | async-start | bytes 294912
  420.5 131.7 %reduce-scatter.23.cloned.1.call-start = ((), (), s32[]{:S(2)}) async-start(), calls=%async_computation.11 | async-start | bytes 294912 | tf_op jit(solution)/shard_map/reduce_scatter | solution.py:118
  428.6 160.5 %reduce-scatter.21.cloned.1.call-start = ((), (), s32[]{:S(2)}) async-start(), calls=%async_computation.10 | async-start | bytes 294912 | tf_op jit(solution)/shard_map/reduce_scatter | solution.py:118
  436.7 257.6 %all-reduce.37.cloned.1.call-start = ((), (), s32[]{:S(2)}) async-start(), calls=%async_computation.16 | async-start | bytes 249856 | tf_op jit(solution)/shard_map/psum | solution.py:114
  589.1 106.2 %reduce-scatter.19.cloned.1.call-start = ((), (), s32[]{:S(2)}) async-start(), calls=%async_computation.9 | async-start | bytes 1179648 | tf_op jit(solution)/shard_map/reduce_scatter | solution.py:117
  600.8 11.5 %copy-start.10 = (f32[6,8192]{1,0:T(8,128)S(1)}, f32[6,8192]{1,0:T(8,128)}, u32[]{:S(2)}) copy-start(f32[6,8192]{1,0:T(8,128)} %copy-done.9) | copy-start | bytes 589828
  600.8 11.5 %copy-start.12 = (f32[6,8192]{1,0:T(8,128)S(1)}, f32[6,8192]{1,0:T(8,128)}, u32[]{:S(2)}) copy-start(f32[6,8192]{1,0:T(8,128)} %copy-done.11) | copy-start | bytes 589828
  600.8 16.4 %copy-start.45 = (bf16[1,512,54]{1,2,0:T(8,128)(2,1)S(1)}, bf16[1,512,54]{1,2,0:T(8,128)(2,1)}, u32[]{:S(2)}) copy-start(bf16[1,512,54]{1,2,0:T(8,128)(2,1)} %copy.118) | copy-start | bytes 165892
  600.9 106.3 %reduce-scatter.17.cloned.1.call-start = ((), (), s32[]{:S(2)}) async-start(), calls=%async_computation.8 | async-start | bytes 1179648 | tf_op jit(solution)/shard_map/reduce_scatter | solution.py:117
  612.3 132.7 %all-reduce.39.cloned.1.call-start = ((), (), s32[]{:S(2)}) async-start(), calls=%async_computation.17 | async-start | bytes 524288 | tf_op jit(solution)/shard_map/psum | solution.py:114
  617.3 7.4 copy-start.27
  617.3 7.8 %copy-start.8 = (f32[12,8192]{1,0:T(8,128)S(1)}, f32[12,8192]{1,0:T(8,128)}, u32[]{:S(2)}) copy-start(f32[12,8192]{1,0:T(8,128)} %copy-done.7) | copy-start | bytes 1179652
  617.3 7.8 %copy-start.55 = (f32[12,12]{1,0:T(8,128)S(1)}, f32[12,12]{1,0:T(8,128)}, u32[]{:S(2)}) copy-start(f32[12,12]{1,0:T(8,128)} %copy-done.54) | copy-start | bytes 1732
  617.3 7.8 %copy-start.71 = (f32[12]{0:T(128)S(1)}, f32[12]{0:T(128)}, u32[]{:S(2)}) copy-start(f32[12]{0:T(128)} %copy-done.70) | copy-start | bytes 148
  623.4 6.7 copy-start.3
  623.4 21.2 %copy-start.23 = (f32[6,8192]{1,0:T(8,128)S(1)}, f32[6,8192]{1,0:T(8,128)}, u32[]{:S(2)}) copy-start(f32[6,8192]{1,0:T(8,128)} %copy-done.22) | copy-start | bytes 589828
  623.4 65.5 %copy-start.50 = (f32[2,12,15]{1,2,0:T(8,128)S(1)}, f32[2,12,15]{1,2,0:T(8,128)}, u32[]{:S(2)}) copy-start(f32[2,12,15]{1,2,0:T(8,128)} %copy-done.49) | copy-start | bytes 4324
  623.4 70.9 %copy-start.48 = (f32[2,64,54]{1,0,2:T(2,128)S(1)}, f32[2,64,54]{1,0,2:T(2,128)}, u32[]{:S(2)}) copy-start(f32[2,64,54]{1,0,2:T(2,128)} %param.31) | copy-start | bytes 82948
  623.5 70.9 %copy-start.61 = (f32[2,64,54]{1,0,2:T(2,128)S(1)}, f32[2,64,54]{1,0,2:T(2,128)}, u32[]{:S(2)}) copy-start(f32[2,64,54]{1,0,2:T(2,128)} %param.43) | copy-start | bytes 82948
  623.5 87.0 %copy-start.44 = (f32[2,108,64]{1,2,0:T(8,128)S(1)}, f32[2,108,64]{1,2,0:T(8,128)}, u32[]{:S(2)}) copy-start(f32[2,108,64]{1,2,0:T(8,128)} %param.33) | copy-start | bytes 165892
  623.5 87.0 %copy-start.58 = (f32[2,108,64]{1,2,0:T(8,128)S(1)}, f32[2,108,64]{1,2,0:T(8,128)}, u32[]{:S(2)}) copy-start(f32[2,108,64]{1,2,0:T(8,128)} %param.45) | copy-start | bytes 165892
  623.9 86.6 %copy-start.59 = (f32[2,108,64]{1,2,0:T(8,128)S(1)}, f32[2,108,64]{1,2,0:T(8,128)}, u32[]{:S(2)}) copy-start(f32[2,108,64]{1,2,0:T(8,128)} %param.39) | copy-start | bytes 165892
  (30 other events, 93.0 us)
Sparse Core Ops, SparseCore 0:
  343.3 33.6 reduce-scatter.30
  406.9 33.5 reduce-scatter.28
  444.1 33.5 reduce-scatter.26
  481.5 33.6 reduce-scatter.24
  518.6 33.5 reduce-scatter.22
  555.4 33.6 reduce-scatter.20
  593.0 34.8 all-reduce.36
  631.4 36.1 reduce-scatter.18
  671.1 36.0 reduce-scatter.16
  709.5 35.4 all-reduce.38
where the time goes:
time: 767 us; the launch traced here: 755 us
  waiting for transfers between devices  192 us (25%)
  blocking collectives  165 us (22%)
  matrix products  156 us (20%)
  local copies, waits for them, and re-layouts  138 us (18%)
  other arithmetic  78.6 us (10%)
  between operations  24.7 us (3%)
    psum x2, blocking collectives, shards(): lax.psum((jnp.sum(state, axis=1), jnp.sum(state * state, axis=1), likely...  79.5 us
    unnamed x14, waiting for transfers between devices  74.3 us
    reduce_scatter x2, waiting for transfers between devices, reduce_layer(): lax.psum_scatter(totals[2], 'wide', scatter_dimension=1, tiled=True)  72.4 us
    concatenate x2, local copies, waits for them, and re-layouts, backward_layer(): jnp.concatenate([shifted_back(low_output, row_step, col_step) for row_ste...  46.5 us
    psum x2, waiting for transfers between devices, reduce_layer(): totals = lax.psum((grads[0], grads[1], grads[2], grads[3]), 'narrow')  33.1 us
    concatenate x3, local copies, waits for them, and re-layouts, all_taps(): jnp.concatenate([shifted(values, row_step, col_step) for row_step, col_st...  30.1 us
    all_gather x2, blocking collectives, fetch_forward(): lax.all_gather(sent[2][layer], 'wide', axis=1, tiled=True)  29.3 us
    unnamed x189, local copies, waits for them, and re-layouts  23.1 us
  transfers between devices with their start and end apart: 10, of which 7 were waited for; matrix products, arithmetic and copies ran while one was open for 21% of the time, Pallas kernels for 0%

commit v1 on v0

v1 whole, which is shorter than its diff:
```python
import functools
import math

import jax
import jax.numpy as jnp
from jax import lax
from jax.experimental import pallas as pl
from jax.experimental.pallas import tpu as pltpu
from jax.sharding import PartitionSpec as P

f32 = jnp.float32
bf16 = jnp.bfloat16
highest = lax.Precision.HIGHEST
MESH = pl.DeviceIdType.MESH
learn_rate = 0.02
beta_one = 0.9
beta_two = 0.999
epsilon = 1e-08
decay_rate = 0.01
penalty_weight = 0.5
tap_offsets = [(r, c) for r in (-1, 0, 1) for c in (-1, 0, 1)]
TILE = 512
BACK = 512
OUT = 144
SMALL = 256
VMEM = pl.BlockSpec(memory_space=pltpu.VMEM)
SMEM = pl.BlockSpec(memory_space=pltpu.SMEM)


def dot(a, b, precision=None):
    return lax.dot_general(
        a, b, (((1,), (0,)), ((), ())), preferred_element_type=f32, precision=precision
    )


def dot_nt(a, b, precision=None):
    return lax.dot_general(
        a, b, (((1,), (1,)), ((), ())), preferred_element_type=f32, precision=precision
    )


def dot_tn(a, b, precision=None):
    return lax.dot_general(
        a, b, (((0,), (0,)), ((), ())), preferred_element_type=f32, precision=precision
    )


def iota(shape, axis):
    return lax.broadcasted_iota(jnp.int32, shape, axis)


def slot(s):
    return s + 2 * ((s * 10923) >> 16)


def spread(count, width, first=0):
    return jnp.where(slot(iota((count, width), 0) + first) == iota((count, width), 1), 1.0, 0.0)


def spread_rows(height, count):
    return jnp.where(slot(iota((height, count), 1)) == iota((height, count), 0), 1.0, 0.0)


def split_three(v):
    high = v.astype(bf16).astype(f32)
    rest = v - high
    middle = rest.astype(bf16).astype(f32)
    return high, middle, rest - middle


def as_row(column):
    n = column.shape[0]
    eye = iota((n, n), 0) == iota((n, n), 1)
    return jnp.sum(jnp.where(eye, column, 0.0), axis=0, keepdims=True)


def mixing_parts(lu):
    n = lu.shape[0]
    row, col = iota((n, n), 0), iota((n, n), 1)
    lower = jnp.where(row > col, lu, 0.0) + jnp.where(row == col, 1.0, 0.0)
    upper = jnp.where(row < col, lu, 0.0) + jnp.where(row == col, jnp.exp(lu), 0.0)
    return lower, upper


def wide_rows(v, lanes):
    return jnp.concatenate([v] * (lanes // 128), axis=1)


class Shifts:
    def __init__(self, mask_ref, lanes):
        self.lanes = lanes
        self.masks = mask_ref

    def mask(self, which, rows):
        m = self.masks[which, :, 0 : self.lanes]
        return jnp.concatenate([m] * (rows // 8), axis=0) if rows > 8 else m

    def col(self, v, c):
        if c == 0:
            return v
        moved = pltpu.roll(v, (-c) % self.lanes, 1)
        return moved * self.mask(0 if c > 0 else 1, v.shape[0])

    def row(self, v, r):
        if r == 0:
            return v
        moved = pltpu.roll(v, (-16 * r) % self.lanes, 1)
        return moved * self.mask(2 if r > 0 else 3, v.shape[0])

    def taps(self, v, sign=1):
        by_col = {c: self.col(v, c) for c in (-1, 0, 1)}
        return [self.row(by_col[sign * c], sign * r) for r, c in tap_offsets]

    def fold(self, pieces, sign=1):
        total = None
        for c in (-1, 0, 1):
            part = None
            for r in (-1, 0, 1):
                piece = self.row(pieces[3 * (r + 1) + (c + 1)], sign * r)
                part = piece if part is None else part + piece
            part = self.col(part, sign * c)
            total = part if total is None else total + part
        return total


def fill_masks(mask_ref):
    lanes = mask_ref.shape[2]
    pos = iota((8, lanes), 1)
    row, col = (pos >> 4) & 15, pos & 15
    for which, keep in enumerate((col < 15, col > 0, row < 15, row > 0)):
        mask_ref[which] = jnp.where(keep, 1.0, 0.0)


def flow_kernel(
    wide,
    narrow,
    pixels_ref,
    noise_ref,
    depth_ref,
    small_ref,
    prior_ref,
    in_ref,
    mid_ref,
    out_ref,
    bias_ref,
    grad_ref,
    sums_ref,
    wall,
    wmt,
    wst,
    win,
    bone,
    mixes,
    mixes_back,
    prior_fwd,
    prior_back,
    masks,
    states,
    keep,
    taps_in,
    hidden_one,
    hidden_two,
    gz,
    stat_acc,
    like_acc,
    prior_acc,
    small_acc,
    bone_acc,
    gst,
    gall,
    rs_buf,
    nr_buf,
    st_wide,
    st_narrow,
    sm_wide,
    sm_narrow,
    ga_send,
    ga_recv,
    rs_send,
    rs_recv,
    nr_send,
    nr_recv,
    st_send,
    st_recv,
    sn_send,
    sn_recv,
    sw_send,
    sw_recv,
    so_send,
    so_recv,
):
    layers, share, hid = mid_ref.shape
    count = pixels_ref.shape[1]
    total = count * wide * narrow
    coeff = -1.0 / (total * 12 * math.log(2.0))
    me_w = lax.axis_index("wide") if wide > 1 else 0
    me_n = lax.axis_index("narrow") if narrow > 1 else 0

    def block(index):
        return pl.ds(pl.multiple_of(index * share, share), share)

    def peer(axis, size, me, d):
        return {axis: lax.rem(me + d, size)}

    def source(size, me, d):
        return lax.rem(me + size - d, size)

    def each(size, fn):
        if size > 1:
            lax.fori_loop(1, size, lambda d, c: (fn(d), c)[1], 0)

    def remote(src, dst, send, recv, device):
        return pltpu.make_async_remote_copy(
            src_ref=src, dst_ref=dst, send_sem=send, recv_sem=recv, device_id=device, device_id_type=MESH
        )

    if wide > 1:
        barrier = pltpu.get_barrier_semaphore()
        each(
            wide,
            lambda d: pl.semaphore_signal(
                barrier, inc=1, device_id=peer("wide", wide, me_w, d), device_id_type=MESH
            ),
        )
        each(
            narrow,
            lambda d: pl.semaphore_signal(
                barrier, inc=1, device_id=peer("narrow", narrow, me_n, d), device_id_type=MESH
            ),
        )

    place = spread(164, SMALL).astype(bf16)
    for layer in range(layers):
        small_part = (
            dot_tn(out_ref[layer].astype(bf16), place[0:108])
            + dot(in_ref[layer].astype(bf16), place[108:162])
            + dot_tn(bias_ref[layer].astype(bf16), place[162:164])
        )
        wall[layer, block(me_w), 0:hid] = mid_ref[layer].astype(bf16)
        wall[layer, block(me_w), hid : hid + SMALL] = small_part.astype(bf16)

    def gather(layer, d):
        mine = wall.at[layer, block(me_w)]
        return remote(
            mine, mine, ga_send.at[layer, d], ga_recv.at[layer, d], peer("wide", wide, me_w, d)
        )

    def gathered(layer, d):
        theirs = wall.at[layer, block(source(wide, me_w, d))]
        return remote(
            theirs, theirs, ga_send.at[layer, d], ga_recv.at[layer, d], peer("wide", wide, me_w, d)
        )

    if wide > 1:
        pl.semaphore_wait(barrier, wide + narrow - 2)
        for layer in range(layers):
            each(wide, lambda d: gather(layer, d).start())

    fill_masks(masks)
    to_slots = spread_rows(16, 12)
    reverse = jnp.where(slot(11 - iota((16, 12), 1)) == iota((16, 12), 0), 1.0, 0.0)
    for layer in range(layers):
        small = small_ref[layer]
        lower, upper = mixing_parts(small[:, 0:12])
        scale = jnp.exp(small[:, 13:14])
        mixed = dot(reverse, dot(lower, upper, highest), highest) * as_row(scale)
        const = jnp.sum(mixed * as_row(small[:, 12:13]), axis=1, keepdims=True)
        back = dot_nt(to_slots, mixed, highest)
        cb = jnp.sum(to_slots * as_row(small[:, 14:15]), axis=1, keepdims=True)
        for c in range(12):
            mixes[layer, c] = jnp.broadcast_to(mixed[:, c : c + 1], (16, 128))
            at = c + 2 * (c // 6)
            mixes_back[layer, c] = jnp.broadcast_to(back[:, at : at + 1], (16, 128))
        mixes[layer, 12] = jnp.broadcast_to(const, (16, 128))
        mixes[layer, 13] = jnp.broadcast_to(cb, (16, 128))

    prior = prior_ref[...]
    s = iota((55, 256), 0)
    at = iota((55, 256), 1)
    hit = (slot(s) == at) | (slot(s) + 72 == at) | (slot(s) + 144 == at)
    to_taps = jnp.where(((s < 54) & hit) | ((s == 54) & (at == 216)), 1.0, 0.0)
    prior_slots = dot(to_slots, prior, highest)
    parts = split_three(dot(prior_slots, to_taps, highest))
    prior_fwd[...] = jnp.concatenate(parts, axis=0).astype(bf16)
    turned = dot_nt(spread_rows(72, 55), prior_slots, highest)
    stacked = jnp.concatenate(list(split_three(turned)) + [jnp.zeros((8, 16), f32)], axis=0)
    again = jnp.where((iota((16, 48), 1) & 15) == iota((16, 48), 0), 1.0, 0.0)
    prior_back[...] = dot(stacked.astype(bf16), again.astype(bf16)).astype(bf16)

    stat_acc[...] = jnp.zeros_like(stat_acc)
    like_acc[...] = jnp.zeros_like(like_acc)
    prior_acc[...] = jnp.zeros_like(prior_acc)
    small_acc[...] = jnp.zeros_like(small_acc)
    bone_acc[...] = jnp.zeros_like(bone_acc)
    gst[...] = jnp.zeros_like(gst)
    gall[...] = jnp.zeros_like(gall)

    def land(size, fn_send, fn_recv):
        def one(d):
            fn_send(d).wait_send()
            fn_recv(d).wait_recv()

        each(size, one)

    pick = jnp.where(iota((SMALL, 128), 0) == iota((SMALL, 128), 1) + OUT, 1.0, 0.0).astype(bf16)
    for layer in range(layers):
        land(wide, functools.partial(gather, layer), functools.partial(gathered, layer))
        wmt[layer] = wall[layer, :, 0:hid].T
        wsm = wall[layer, :, hid : hid + SMALL]
        wst[layer] = wsm.T
        win[layer] = dot(wsm, pick).astype(bf16)
        bone[layer] = jnp.broadcast_to(wsm[:, 217:218].astype(f32), (hid, 128))

    def by_lanes(v):
        total_lanes = v[:, 0:128]
        for k in range(1, v.shape[1] // 128):
            total_lanes = total_lanes + v[:, 128 * k : 128 * k + 128]
        return total_lanes

    real = jnp.where(iota((8, 128), 0) < 6, 1.0, 0.0)

    def forward(t, carry):
        here = pl.ds(pl.multiple_of(t * TILE, TILE), TILE)
        shifts = Shifts(masks, TILE)
        images = TILE // 256
        blank = jnp.zeros((2, 256), f32)
        chunks = []
        for k in range(images):
            coarse = depth_ref[t * images + k] == 5
            by = jnp.where(coarse, 3, 0)
            level = jnp.where(coarse, 1.0 / 32.0, 1.0 / 256.0).astype(f32)
            at_image = pl.ds(pl.multiple_of(t * TILE + k * 256, 256), 256)
            quant = lax.shift_right_logical(pixels_ref[:, at_image], jnp.broadcast_to(by, (12, 256)))
            x = (quant.astype(f32) + noise_ref[:, at_image]) * level - 0.5
            chunks.append(jnp.concatenate([x[0:6], blank, x[6:12], blank], axis=0))
        x = jnp.concatenate(chunks, axis=1)
        states[0, :, here] = x
        logs = None
        for layer in range(layers):
            y = wide_rows(mixes[layer, 12], TILE)
            for c in range(12):
                at = c + 2 * (c // 6)
                y = y + wide_rows(mixes[layer, c], TILE) * x[at : at + 1, :]
            kept, other = y[0:8], y[8:16]
            ones = jnp.where(iota((8, TILE), 0) == 0, 1.0, 0.0)
            s0 = jnp.concatenate(shifts.taps(kept) + [ones], axis=0).astype(bf16)
            taps_in[layer, :, here] = s0
            h1 = jnp.maximum(dot(win[layer, :, 0:80], s0), 0.0).astype(bf16)
            hidden_one[layer, :, here] = h1
            second = dot(wall[layer, :, 0:hid], h1) + wide_rows(bone[layer], TILE)
            h2 = jnp.maximum(second, 0.0).astype(bf16)
            hidden_two[layer, :, here] = h2
            taps_out = dot(wst[layer, 0:OUT, :], h2)
            o = shifts.fold([taps_out[16 * k : 16 * k + 16] for k in range(9)])
            o = o + wide_rows(mixes[layer, 13], TILE)
            v = other + o[0:8]
            decay = 1.0 + jnp.exp(-(o[8:16] + 2.0))
            q = 1.0 / decay
            term = by_lanes(jnp.log(decay))
            logs = term if logs is None else logs + term
            keep[layer, 0:8, here] = v
            keep[layer, 8:16, here] = q
            x = jnp.concatenate([kept, v * q], axis=0)
            states[layer + 1, :, here] = x
        stat_acc[0] += by_lanes(x)
        stat_acc[1] += by_lanes(x * x)
        like_acc[...] -= logs * real
        return carry

    lax.fori_loop(0, count // TILE, forward, 0)

    lane = iota((16, 128), 1)
    stats = jnp.where(lane == 0, jnp.sum(stat_acc[0], axis=1, keepdims=True), 0.0) + jnp.where(
        lane == 1, jnp.sum(stat_acc[1], axis=1, keepdims=True), 0.0
    )
    st_wide[me_w] = stats

    def stat_send(d):
        mine = st_wide.at[me_w]
        return remote(mine, mine, st_send.at[d], st_recv.at[d], peer("wide", wide, me_w, d))

    def stat_recv(d):
        theirs = st_wide.at[source(wide, me_w, d)]
        return remote(theirs, theirs, st_send.at[d], st_recv.at[d], peer("wide", wide, me_w, d))

    each(wide, lambda d: stat_send(d).start())

    def prior_tile(t, carry):
        here = pl.ds(pl.multiple_of(t * TILE, TILE), TILE)
        shifts = Shifts(masks, TILE)
        z1 = states[layers, 0:8, here]
        z2 = states[layers, 8:16, here]
        ones = jnp.where(iota((8, TILE), 0) == 0, 1.0, 0.0)
        pieces = [split_three(v) for v in shifts.taps(z1)]
        tz = jnp.concatenate(
            [p[0] for p in pieces] + [p[1] for p in pieces] + [p[2] for p in pieces] + [ones], axis=0
        ).astype(bf16)
        three = dot(prior_fwd[:, 0:224], tz)
        stat = three[0:16] + three[16:32] + three[32:48]
        centre, log_sd = stat[0:8], stat[8:16]
        inverse = jnp.exp(-log_sd)
        ratio = (z2 - centre) * inverse
        like_acc[...] += by_lanes(-0.5 * z1 * z1 - 0.5 * ratio * ratio - log_sd)
        d_centre = ratio * inverse
        d_stat = jnp.concatenate([d_centre, ratio * ratio - 1.0], axis=0)
        ds = jnp.concatenate(split_three(d_stat), axis=0).astype(bf16)
        prior_acc[:, 0:224] += dot_nt(ds, tz)
        dt = dot(prior_back[...], ds)
        dt = dt[0:72] + dt[72:144] + dt[144:216]
        folded = shifts.fold([dt[8 * k : 8 * k + 8] for k in range(9)], -1)
        gz[0:8, here] = coeff * (folded - z1)
        gz[8:16, here] = -coeff * d_centre
        return carry

    lax.fori_loop(0, count // TILE, prior_tile, 0)

    land(wide, stat_send, stat_recv)
    stats = st_wide[0]
    for k in range(1, wide):
        stats = stats + st_wide[k]
    st_narrow[me_n] = stats

    def stat_send_n(d):
        mine = st_narrow.at[me_n]
        return remote(mine, mine, sn_send.at[d], sn_recv.at[d], peer("narrow", narrow, me_n, d))

    def stat_recv_n(d):
        theirs = st_narrow.at[source(narrow, me_n, d)]
        return remote(theirs, theirs, sn_send.at[d], sn_recv.at[d], peer("narrow", narrow, me_n, d))

    each(narrow, lambda d: stat_send_n(d).start())
    land(narrow, stat_send_n, stat_recv_n)
    stats = st_narrow[0]
    for k in range(1, narrow):
        stats = stats + st_narrow[k]
    mean = stats[:, 0:1] / total
    var = stats[:, 1:2] / total - mean * mean
    from_first = penalty_weight * (2.0 * mean - 4.0 * (var - 1.0) * mean) / total
    from_square = penalty_weight * 2.0 * (var - 1.0) / total
    ones_rows = jnp.where((iota((16, 1), 0) & 7) < 6, 1.0, 0.0)
    penalty = penalty_weight * jnp.sum(
        ones_rows * (mean * mean + (var - 1.0) * (var - 1.0)), axis=0, keepdims=True
    )

    def backward(layer):
        def tile(t, carry):
            here = pl.ds(pl.multiple_of(t * BACK, BACK), BACK)
            shifts = Shifts(masks, BACK)
            g = gz[:, here]
            if layer == layers - 1:
                g = g + from_first + 2.0 * states[layers, :, here] * from_square
            ga, gb = g[0:8], g[8:16]
            v = keep[layer, 0:8, here]
            q = keep[layer, 8:16, here]
            gbq = gb * q
            do = jnp.concatenate([gbq, (gbq * v + coeff) * (1.0 - q)], axis=0)
            rounded = do.astype(bf16).astype(f32)
            d3 = jnp.concatenate(shifts.taps(rounded, -1), axis=0).astype(bf16)
            h2 = hidden_two[layer, :, here]
            gst[layer, 0:OUT, :] += dot_nt(d3, h2)
            dd2 = dot(wall[layer, :, hid : hid + OUT], d3)
            masked = jnp.where(h2 > 0, dd2, 0.0)
            bone_acc[layer] += by_lanes(masked)
            d2 = masked.astype(bf16)
            h1 = hidden_one[layer, :, here]
            gall[layer, :, 0:hid] += dot_nt(d2, h1)
            dd1 = dot(wmt[layer], d2)
            d1 = jnp.where(h1 > 0, dd1, 0.0).astype(bf16)
            s0 = taps_in[layer, :, here]
            gst[layer, OUT : OUT + 80, :] += dot_nt(s0, d1)
            dt = dot(wst[layer, OUT : OUT + 80, :], d1)
            gya = ga + shifts.fold([dt[8 * k : 8 * k + 8] for k in range(9)], -1)
            gy = jnp.concatenate([gya, gbq], axis=0)
            x = states[layer, :, here]
            ones = jnp.where(iota((16, BACK), 0) == 0, 1.0, 0.0)
            left = jnp.concatenate(split_three(gy) + split_three(do), axis=0).astype(bf16)
            right = jnp.concatenate(split_three(x) + (ones,), axis=0).astype(bf16)
            small_acc[layer, :, 0:64] += dot_nt(left, right)
            if layer:
                gx = wide_rows(mixes_back[layer, 0], BACK) * gy[0:1, :]
                for c in range(1, 12):
                    at = c + 2 * (c // 6)
                    gx = gx + wide_rows(mixes_back[layer, c], BACK) * gy[at : at + 1, :]
                gz[:, here] = gx
            return carry

        lax.fori_loop(0, count // BACK, tile, 0)
        column = jnp.sum(bone_acc[layer], axis=1, keepdims=True)
        gall[layer, :, hid : hid + SMALL] = gst[layer].T + jnp.where(
            iota((hid, SMALL), 1) == 217, column, 0.0
        )

    def rs_go(layer, d):
        to = lax.rem(me_w + d, wide)
        return remote(
            gall.at[layer, block(to)],
            rs_buf.at[layer, d],
            rs_send.at[layer, d],
            rs_recv.at[layer, d],
            {"wide": to},
        )

    def nr_go(layer, d):
        mine = nr_buf.at[layer, me_n]
        return remote(
            mine, mine, nr_send.at[layer, d], nr_recv.at[layer, d], peer("narrow", narrow, me_n, d)
        )

    def nr_come(layer, d):
        theirs = nr_buf.at[layer, source(narrow, me_n, d)]
        return remote(
            theirs, theirs, nr_send.at[layer, d], nr_recv.at[layer, d], peer("narrow", narrow, me_n, d)
        )

    def rs_end(layer):
        land(wide, functools.partial(rs_go, layer), functools.partial(rs_go, layer))
        nr_buf[layer, me_n] = gall[layer, block(me_w), :]

        def add(d):
            nr_buf[layer, me_n] += rs_buf[layer, d]

        each(wide, add)
        each(narrow, lambda d: nr_go(layer, d).start())

    def nr_end(layer):
        land(narrow, functools.partial(nr_go, layer), functools.partial(nr_come, layer))
        whole = nr_buf[layer, 0]
        for k in range(1, narrow):
            whole = whole + nr_buf[layer, k]
        grad_ref[layer] = whole

    for layer in reversed(range(layers)):
        backward(layer)
        each(wide, lambda d: rs_go(layer, d).start())

    pieces = []
    for layer in range(layers):
        acc = small_acc[layer]
        gy_part = acc[0:16] + acc[16:32] + acc[32:48]
        do_part = acc[48:64] + acc[64:80] + acc[80:96]
        moment = gy_part + pltpu.roll(gy_part, 112, 1) + pltpu.roll(gy_part, 96, 1)
        moment = jnp.where(lane < 16, moment, 0.0)
        moment = moment + jnp.where(lane == 16, pltpu.roll(gy_part, 96, 1), 0.0)
        moment = moment + jnp.where(lane == 17, pltpu.roll(do_part, 97, 1), 0.0)
        pieces.append(moment)
    acc = prior_acc[0:16] + prior_acc[16:32] + prior_acc[32:48]
    taps_part = (
        acc + pltpu.roll(acc, 256 - 72, 1) + pltpu.roll(acc, 256 - 144, 1)
    )[:, 0:128]
    ones_part = pltpu.roll(acc, 256 - 144, 1)[:, 0:128]
    pieces.append(jnp.where(lane < 72, taps_part, 0.0) + jnp.where(lane == 72, ones_part, 0.0))
    depths = lax.fori_loop(0, depth_ref.shape[0], lambda k, c: c + depth_ref[k], jnp.int32(0))
    depths = jnp.broadcast_to(depths, (8, 128)).astype(f32)
    row8 = iota((8, 128), 0)
    logs = jnp.sum(like_acc[...], axis=0, keepdims=True)
    pieces.append(jnp.where(row8 == 0, logs, 0.0) + jnp.where(row8 == 1, depths, 0.0))
    sm_wide[me_w] = jnp.concatenate(pieces, axis=0)

    def sw_go(d):
        mine = sm_wide.at[me_w]
        return remote(mine, mine, sw_send.at[d], sw_recv.at[d], peer("wide", wide, me_w, d))

    def sw_come(d):
        theirs = sm_wide.at[source(wide, me_w, d)]
        return remote(theirs, theirs, sw_send.at[d], sw_recv.at[d], peer("wide", wide, me_w, d))

    def so_go(d):
        mine = sm_narrow.at[me_n]
        return remote(mine, mine, so_send.at[d], so_recv.at[d], peer("narrow", narrow, me_n, d))

    def so_come(d):
        theirs = sm_narrow.at[source(narrow, me_n, d)]
        return remote(theirs, theirs, so_send.at[d], so_recv.at[d], peer("narrow", narrow, me_n, d))

    each(wide, lambda d: sw_go(d).start())
    land(wide, sw_go, sw_come)
    whole = sm_wide[0]
    for k in range(1, wide):
        whole = whole + sm_wide[k]
    sm_narrow[me_n] = whole
    each(narrow, lambda d: so_go(d).start())
    for layer in reversed(range(layers)):
        rs_end(layer)
    land(narrow, so_go, so_come)
    whole = sm_narrow[0]
    for k in range(1, narrow):
        whole = whole + sm_narrow[k]
    rows = whole.shape[0]
    sums_ref[...] = whole + jnp.where(iota((rows, 128), 0) == rows - 8 + 2, penalty, 0.0)
    for layer in reversed(range(layers)):
        nr_end(layer)


def adamw(weight, grad, first, second, fixes):
    first_new = beta_one * first + (1.0 - beta_one) * grad
    second_new = beta_two * second + (1.0 - beta_two) * grad * grad
    update = first_new / fixes[0] / (jnp.sqrt(second_new / fixes[1]) + epsilon) + decay_rate * weight
    return (weight - learn_rate * update, first_new, second_new)


def update_kernel(total, images, step_ref, grad_ref, sums_ref, *refs):
    weights, firsts, seconds, loss_ref, outs = refs[0:6], refs[6:12], refs[12:18], refs[18], refs[19:]
    layers, share, _ = grad_ref.shape
    hid = weights[1].shape[2]
    coeff = -1.0 / (total * 12 * math.log(2.0))
    power = iota((8, 128), 1)
    used = power < jnp.broadcast_to(step_ref[0], (8, 128))
    fixes = tuple(
        (1.0 - beta)
        * jnp.sum(
            jnp.where(used, jnp.exp(power.astype(f32) * math.log(beta)), 0.0), axis=1, keepdims=True
        )[0:1]
        for beta in (beta_one, beta_two)
    )

    def write(which, at, grad):
        new = adamw(weights[which][at], grad, firsts[which][at], seconds[which][at], fixes)
        for k in range(3):
            outs[3 * which + k][at] = new[k]

    place = spread(164, SMALL)
    to_slots = spread_rows(16, 12)
    reverse = jnp.where(slot(11 - iota((16, 12), 1)) == iota((16, 12), 0), 1.0, 0.0)
    row, col = iota((12, 12), 0), iota((12, 12), 1)
    eye = row == col
    logdet = jnp.zeros((1, 1), f32)
    for layer in range(layers):
        write(1, layer, grad_ref[layer, :, 0:hid])
        part = grad_ref[layer, :, hid : hid + SMALL]
        write(0, layer, dot_nt(part, place[108:162], highest))
        write(2, layer, dot_nt(place[0:108], part, highest))
        write(3, layer, dot_nt(place[162:164], part, highest))
        small = weights[4][layer]
        lu = small[:, 0:12]
        lower, upper = mixing_parts(lu)
        scale = jnp.exp(small[:, 13:14])
        scale_row = as_row(scale)
        sums = sums_ref[16 * layer : 16 * layer + 16]
        turned = dot_tn(reverse, sums, highest)
        moment = dot(turned[:, 0:16], to_slots, highest)
        ones = turned[:, 16:17]
        g_mix = (moment + ones * as_row(small[:, 12:13])) * scale_row
        mix = dot(lower, upper, highest)
        g_bias = scale * dot_tn(mix, ones, highest)
        g_scale = as_column(jnp.sum(mix * g_mix, axis=0, keepdims=True)) + coeff * total
        g_lower = dot_nt(g_mix, upper, highest)
        g_upper = dot_tn(lower, g_mix, highest)
        g_lu = jnp.where(row > col, g_lower, jnp.where(eye, g_upper * jnp.exp(lu) + coeff * total, g_upper))
        g_cb = dot_tn(to_slots, sums, highest)[:, 17:18]
        wide15 = iota((12, 15), 1)
        grad = dot(g_lu, jnp.where(iota((12, 15), 0) == wide15, 1.0, 0.0), highest)
        grad = jnp.where(wide15 == 12, g_bias, grad)
        grad = jnp.where(wide15 == 13, g_scale, grad)
        grad = jnp.where(wide15 == 14, g_cb, grad)
        write(4, layer, grad)
        diag = jnp.sum(jnp.where(eye, lu, 0.0), axis=0, keepdims=True) + as_row(small[:, 13:14])
        logdet = logdet + jnp.sum(diag, axis=1, keepdims=True)
    sums = sums_ref[16 * layers : 16 * layers + 16]
    grad = coeff * dot_nt(
        dot_tn(to_slots, sums, highest), spread(55, 128), highest
    )
    write(5, Ellipsis, grad)
    tail = sums_ref[16 * layers + 16 :]
    likely = jnp.sum(tail[0:1], axis=1, keepdims=True)
    likely = likely - total * 6.0 * math.log(2.0 * math.pi) + total * logdet
    loss_ref[...] = coeff * likely + tail[1:2, 0:1] / images + tail[2:3, 0:1]


def as_column(row):
    n = row.shape[1]
    eye = iota((n, n), 0) == iota((n, n), 1)
    return jnp.sum(jnp.where(eye, row, 0.0), axis=1, keepdims=True)


def shards(*args, wide, narrow):
    pixels, noise, depth, step_count = args[0:4]
    params, firsts, seconds = args[4:10], args[10:16], args[16:22]
    layers, share, hid = params[1].shape
    count = pixels.shape[1]
    width = hid + SMALL
    rows = 16 * layers + 16 + 8
    dma = pltpu.SemaphoreType.DMA
    big = functools.partial(pltpu.VMEM)
    scratch = [
        big((layers, hid, width), bf16),
        big((layers, hid, hid), bf16),
        big((layers, SMALL, hid), bf16),
        big((layers, hid, 128), bf16),
        big((layers, hid, 128), f32),
        big((layers, 14, 16, 128), f32),
        big((layers, 12, 16, 128), f32),
        big((48, 256), bf16),
        big((224, 48), bf16),
        big((4, 8, max(TILE, BACK)), f32),
        big((layers + 1, 16, count), f32),
        big((layers, 16, count), f32),
        big((layers, 80, count), bf16),
        big((layers, hid, count), bf16),
        big((layers, hid, count), bf16),
        big((16, count), f32),
        big((2, 16, 128), f32),
        big((8, 128), f32),
        big((48, 256), f32),
        big((layers, 96, 128), f32),
        big((layers, hid, 128), f32),
        big((layers, SMALL, hid), f32),
        big((layers, hid, width), f32),
        big((layers, wide, share, width), f32),
        big((layers, narrow, share, width), f32),
        big((wide, 16, 128), f32),
        big((narrow, 16, 128), f32),
        big((wide, rows, 128), f32),
        big((narrow, rows, 128), f32),
        dma((layers, wide)),
        dma((layers, wide)),
        dma((layers, wide)),
        dma((layers, wide)),
        dma((layers, narrow)),
        dma((layers, narrow)),
        dma((wide,)),
        dma((wide,)),
        dma((narrow,)),
        dma((narrow,)),
        dma((wide,)),
        dma((wide,)),
        dma((narrow,)),
        dma((narrow,)),
    ]
    remote = {"collective_id": 0, "has_side_effects": True} if wide > 1 else {}
    grads, sums = pl.pallas_call(
        functools.partial(flow_kernel, wide, narrow),
        out_shape=(
            jax.ShapeDtypeStruct((layers, share, width), f32),
            jax.ShapeDtypeStruct((rows, 128), f32),
        ),
        in_specs=[VMEM, VMEM, SMEM] + [VMEM] * 6,
        out_specs=(VMEM, VMEM),
        scratch_shapes=scratch,
        compiler_params=pltpu.CompilerParams(vmem_limit_bytes=63 * 1024 * 1024, **remote),
        name="flow",
    )(pixels, noise, depth, params[4], params[5], params[0], params[1], params[2], params[3])
    total = count * wide * narrow
    shapes = [jax.ShapeDtypeStruct((1, 1), f32)]
    for p in params:
        shapes += [jax.ShapeDtypeStruct(p.shape, f32)] * 3
    results = pl.pallas_call(
        functools.partial(update_kernel, total, total // 256),
        out_shape=tuple(shapes),
        in_specs=[SMEM] + [VMEM] * 20,
        out_specs=(VMEM,) * 19,
        compiler_params=pltpu.CompilerParams(vmem_limit_bytes=32 * 1024 * 1024),
        name="update",
    )(step_count.reshape(1), grads, sums, *params, *firsts, *seconds)
    return (results[0].reshape(()),) + tuple(results[1:])


def solution(mesh):
    weights = (P(None, "wide", None), P(None, "wide", None), P(None, None, "wide"), P(None, None, "wide"), P(), P())
    return jax.shard_map(
        functools.partial(shards, wide=mesh.shape["wide"], narrow=mesh.shape["narrow"]),
        mesh=mesh,
        in_specs=(
            P(None, ("narrow", "wide")),
            P(None, ("narrow", "wide")),
            P(("narrow", "wide")),
            P(),
        )
        + weights * 3,
        out_specs=(P(),) + tuple(w for w in weights for _ in range(3)),
        check_vma=False,
    )
```

time: 767 us -> 225 us (0.29); the launches traced: 755 us -> 223 us
  Pallas kernels: 0 us -> 200 us
  waiting for transfers between devices: 192 us -> 0 us
  blocking collectives: 165 us -> 0 us
  matrix products: 156 us -> 0 us
  local copies, waits for them, and re-layouts: 138 us -> 21.6 us
  other arithmetic: 78.6 us -> 0 us
  between operations: 24.7 us -> 1.43 us
    pallas_call x0 -> x2, Pallas kernels: none -> 200 us  [the longest x1 197 us: shards(): pl.pallas_call(functools.partial(flow_kernel, wide, narrow), out_shape=(j...]
    dot_general x31 -> x0, matrix products: 143 us -> none  [the longest x2 23 us: backward_layer(): lax.dot_general(w_second, low_two, contract_first, preferred_element_type...]
    all_gather x8 -> x0, blocking collectives: 85.5 us -> none  [the longest x2 29.3 us: fetch_forward(): lax.all_gather(sent[2][layer], 'wide', axis=1, tiled=True)]
    reduce_scatter x4 -> x0, waiting for transfers between devices: 84.3 us -> none  [the longest x2 72.4 us: reduce_layer(): lax.psum_scatter(totals[2], 'wide', scatter_dimension=1, tiled=True)]
    psum x2 -> x0, blocking collectives: 79.5 us -> none  [shards(): lax.psum((jnp.sum(state, axis=1), jnp.sum(state * state, axis=1), likely...]
    concatenate x5 -> x0, local copies, waits for them, and re-layouts: 76.6 us -> none  [the longest x2 46.5 us: backward_layer(): jnp.concatenate([shifted_back(low_output, row_step, col_step) for row_ste...]
    unnamed x14 -> x0, waiting for transfers between devices: 74.3 us -> none
    psum x2 -> x0, waiting for transfers between devices: 33.1 us -> none  [reduce_layer(): totals = lax.psum((grads[0], grads[1], grads[2], grads[3]), 'narrow')]
  transfers between devices with their start and end apart: 10 -> 0, of which waited for: 7 -> 0; matrix products, arithmetic and copies ran while one was open for 21% -> 0% of each run, Pallas kernels for 0% -> 0%
where the time goes in v1:
time: 225 us; the launch traced here: 223 us
  Pallas kernels  200 us (89%)
  local copies, waits for them, and re-layouts  21.6 us (10%)
    pallas_call x1, Pallas kernels, shards(): pl.pallas_call(functools.partial(flow_kernel, wide, narrow), out_shape=(j...  197 us
    unnamed x62, local copies, waits for them, and re-layouts  21.6 us

profile of v1, /device:TPU:0, one launch (start us, length us, event | category | flops | bytes accessed | tf_op | source)
XLA Modules:
  0.0 223.0 jit_solution(14226526255216895965)
XLA Ops:
  0.7 0.0 copy-start.19
  1.3 1.3 copy.41.small_ref.refs_4_
  2.6 0.7 copy.49.refs_10_
  3.3 0.7 copy.52.refs_16_
  4.1 0.0 copy-done.19
  4.1 0.0 copy-start.20
  4.1 0.7 copy.42.in_ref.refs_0_
  4.8 0.1 copy-done.20
  4.9 0.0 copy-start.21
  4.9 0.7 copy.47.refs_6_
  5.6 0.1 copy-done.21
  5.7 0.0 copy-start.16
  5.7 0.7 copy.50.refs_12_
  6.4 0.1 copy-done.16
  6.5 0.0 copy-start.17
  6.5 0.8 copy.43.out_ref.refs_2_
  7.3 0.1 copy-done.17
  7.4 0.0 copy-start.18
  7.4 0.1 copy.48.refs_8_
  7.5 0.7 copy-done.18
  8.2 0.1 copy.51.refs_14_
  8.3 0.0 copy-start
  8.3 0.0 copy-start.1
  8.3 0.0 copy-start.2
  8.3 0.0 copy-start.4
  8.4 0.0 copy-start.8
  8.4 197.4 %flow.1 = (f32[2,64,768]{2,1,0:T(8,128)}, f32[56,128]{1,0:T(8,128)}) custom-call(s32[12,8192]{1,0:T(8,128)} %pixels_ref.1, f32[12,8192]{1,0:T(8,128)} %noise_ref.1, s32[32]{0:T(128)} %depth_ref.1, f32[2,12,15]{2,1,0:T(8,128)} %copy.41.small_ref.refs_4_, f32[12,55]{1,0:T(8,128)} %refs_5_.1, f32[2,64,54]{2,1,0:T(8,128)} %copy.42.in_ref.refs_0_, ...), custom_call_target="tpu_custom_call" | custom-call | tf_op jit(solution)/shard_map/flow/pallas_call | solution.py:730
  205.7 0.0 copy-start.13
  205.8 0.0 copy-done
  205.8 0.0 copy-done.1
  205.8 0.0 copy-done.2
  205.8 0.0 copy-done.4
  205.8 0.0 copy-done.8
  205.8 0.6 copy-done.13
  206.4 0.0 copy-start.3
  206.4 1.0 copy-done.3
  207.4 0.0 copy-start.5
  207.4 0.9 copy-done.5
  208.4 0.0 copy-start.6
  208.4 0.8 copy-done.6
  209.2 0.0 copy-start.7
  209.2 0.8 copy-done.7
  210.1 0.0 copy-start.9
  210.1 0.7 copy-done.9
  210.8 0.0 copy-start.10
  210.8 0.7 copy-done.10
  211.5 0.0 copy-start.11
  211.5 0.7 copy-done.11
  212.2 0.0 copy-start.12
  212.2 0.7 copy-done.12
  212.9 0.0 copy-start.14
  212.9 0.7 copy-done.14
  213.6 0.0 copy-start.15
  213.6 0.7 copy-done.15
  214.3 2.6 %update.1 = (f32[1,1]{1,0:T(1,128)}, f32[2,64,54]{2,1,0:T(8,128)S(1)}, f32[2,64,54]{2,1,0:T(8,128)S(1)}, f32[2,64,54]{2,1,0:T(8,128)S(1)}, f32[2,64,512]{2,1,0:T...) custom-call(s32[1]{0:T(128)} %bitcast.2.step_ref, ...), custom_call_target="tpu_custom_call" | custom-call | tf_op jit(solution)/shard_map/update/pallas_call | solution.py:746
  216.9 0.7 copy.53
  217.6 0.6 copy.59
  218.2 0.6 copy.60
  218.8 0.6 copy.61
  219.4 0.7 copy.54
  220.1 0.7 copy.55
  220.8 0.7 copy.56
  221.5 0.7 copy.57
  222.3 0.7 copy.58
Async XLA Ops:
  0.7 3.4 %copy-start.19 = (f32[2,64,54]{1,0,2:T(2,128)S(1)}, f32[2,64,54]{1,0,2:T(2,128)}, u32[]{:S(2)}) copy-start(f32[2,64,54]{1,0,2:T(2,128)} %param.26) | copy-start | bytes 82948
  4.1 0.8 copy-start.20
  4.9 0.8 copy-start.21
  5.7 0.8 copy-start.16
  6.5 0.8 copy-start.17
  7.4 0.8 copy-start.18
  8.3 197.4 %copy-start = (f32[2,64,512]{2,1,0:T(8,128)S(1)}, f32[2,64,512]{2,1,0:T(8,128)}, u32[]{:S(2)}) copy-start(f32[2,64,512]{2,1,0:T(8,128)} %refs_1_.1) | copy-start | bytes 786436
  8.3 197.4 %copy-start.1 = (f32[2,108,64]{2,1,0:T(8,128)S(1)}, f32[2,108,64]{2,1,0:T(8,128)}, u32[]{:S(2)}) copy-start(f32[2,108,64]{2,1,0:T(8,128)} %copy.43.out_ref.refs_2_) | copy-start | bytes 165892
  8.3 197.4 %copy-start.2 = (f32[2,64,54]{2,1,0:T(8,128)S(1)}, f32[2,64,54]{2,1,0:T(8,128)}, u32[]{:S(2)}) copy-start(f32[2,64,54]{2,1,0:T(8,128)} %copy.42.in_ref.refs_0_) | copy-start | bytes 82948
  8.3 197.4 %copy-start.4 = (f32[2,64,512]{2,1,0:T(8,128)S(1)}, f32[2,64,512]{2,1,0:T(8,128)}, u32[]{:S(2)}) copy-start(f32[2,64,512]{2,1,0:T(8,128)} %refs_7_.1) | copy-start | bytes 786436
  8.4 197.4 %copy-start.8 = (f32[2,12,15]{2,1,0:T(8,128)S(1)}, f32[2,12,15]{2,1,0:T(8,128)}, u32[]{:S(2)}) copy-start(f32[2,12,15]{2,1,0:T(8,128)} %copy.41.small_ref.refs_4_) | copy-start | bytes 4324
  205.7 0.7 copy-start.13
  206.4 1.0 copy-start.3
  207.4 0.9 copy-start.5
  208.4 0.8 copy-start.6
  209.2 0.8 copy-start.7
  210.1 0.7 copy-start.9
  210.8 0.7 copy-start.10
  211.5 0.7 copy-start.11
  212.2 0.7 copy-start.12
  212.9 0.7 copy-start.14
  213.6 0.7 copy-start.15

commit v2 on v1

v2 whole, which is shorter than its diff:
```python
import functools
import math

import jax
import jax.numpy as jnp
from jax import lax
from jax.experimental import pallas as pl
from jax.experimental.pallas import tpu as pltpu
from jax.sharding import PartitionSpec as P

f32 = jnp.float32
bf16 = jnp.bfloat16
highest = lax.Precision.HIGHEST
MESH = pl.DeviceIdType.MESH
learn_rate = 0.02
beta_one = 0.9
beta_two = 0.999
epsilon = 1e-08
decay_rate = 0.01
penalty_weight = 0.5
tap_offsets = [(r, c) for r in (-1, 0, 1) for c in (-1, 0, 1)]
TILE = 2048
FLOW_VMEM = 60 * 1024 * 1024
UPDATE_VMEM = 60 * 1024 * 1024
OUT = 144
SMALL = 256
VMEM = pl.BlockSpec(memory_space=pltpu.VMEM)
SMEM = pl.BlockSpec(memory_space=pltpu.SMEM)


def dot(a, b, precision=None):
    return lax.dot_general(
        a, b, (((1,), (0,)), ((), ())), preferred_element_type=f32, precision=precision
    )


def dot_nt(a, b, precision=None):
    return lax.dot_general(
        a, b, (((1,), (1,)), ((), ())), preferred_element_type=f32, precision=precision
    )


def dot_tn(a, b, precision=None):
    return lax.dot_general(
        a, b, (((0,), (0,)), ((), ())), preferred_element_type=f32, precision=precision
    )


def iota(shape, axis):
    return lax.broadcasted_iota(jnp.int32, shape, axis)


def slot(s):
    return s + 2 * ((s * 10923) >> 16)


def spread(count, width, first=0):
    return jnp.where(slot(iota((count, width), 0) + first) == iota((count, width), 1), 1.0, 0.0)


def spread_rows(height, count):
    return jnp.where(slot(iota((height, count), 1)) == iota((height, count), 0), 1.0, 0.0)


def split_three(v):
    high = v.astype(bf16).astype(f32)
    rest = v - high
    middle = rest.astype(bf16).astype(f32)
    return high, middle, rest - middle


def as_row(column):
    n = column.shape[0]
    eye = iota((n, n), 0) == iota((n, n), 1)
    return jnp.sum(jnp.where(eye, column, 0.0), axis=0, keepdims=True)


def mixing_parts(lu):
    n = lu.shape[0]
    row, col = iota((n, n), 0), iota((n, n), 1)
    lower = jnp.where(row > col, lu, 0.0) + jnp.where(row == col, 1.0, 0.0)
    upper = jnp.where(row < col, lu, 0.0) + jnp.where(row == col, jnp.exp(lu), 0.0)
    return lower, upper


def wide_rows(v, lanes):
    return jnp.concatenate([v] * (lanes // 128), axis=1)


class Shifts:
    def __init__(self, mask_ref, lanes):
        self.lanes = lanes
        self.masks = mask_ref

    def mask(self, which, rows):
        m = self.masks[which, :, 0 : self.lanes]
        return jnp.concatenate([m] * (rows // 8), axis=0) if rows > 8 else m

    def col(self, v, c):
        if c == 0:
            return v
        moved = pltpu.roll(v, (-c) % self.lanes, 1)
        return moved * self.mask(0 if c > 0 else 1, v.shape[0])

    def row(self, v, r):
        if r == 0:
            return v
        moved = pltpu.roll(v, (-16 * r) % self.lanes, 1)
        return moved * self.mask(2 if r > 0 else 3, v.shape[0])

    def taps(self, v, sign=1):
        by_col = {c: self.col(v, c) for c in (-1, 0, 1)}
        return [self.row(by_col[sign * c], sign * r) for r, c in tap_offsets]

    def fold(self, pieces, sign=1):
        total = None
        for c in (-1, 0, 1):
            part = None
            for r in (-1, 0, 1):
                piece = self.row(pieces[3 * (r + 1) + (c + 1)], sign * r)
                part = piece if part is None else part + piece
            part = self.col(part, sign * c)
            total = part if total is None else total + part
        return total


def fill_masks(mask_ref):
    lanes = mask_ref.shape[2]
    pos = iota((8, lanes), 1)
    row, col = (pos >> 4) & 15, pos & 15
    for which, keep in enumerate((col < 15, col > 0, row < 15, row > 0)):
        mask_ref[which] = jnp.where(keep, 1.0, 0.0)


def flow_kernel(wide, narrow, layout, *refs):
    names, groups = layout
    at = dict(zip(names, refs))
    pixels_ref, noise_ref, depth_ref = at["pixels"], at["noise"], at["depth"]
    wall, wmt, wst, win, bone = at["wall"], at["wmt"], at["wst"], at["win"], at["bone"]
    mixes, mixes_back = at["mixes"], at["mixes_back"]
    states, keep, taps_in, gz = at["states"], at["keep"], at["taps_in"], at["gz"]
    hidden_one, hidden_two = at["hidden_one"], at["hidden_two"]
    layers, share, hid = at["mid"].shape
    count = pixels_ref.shape[1]
    total = count * wide * narrow
    coeff = -1.0 / (total * 12 * math.log(2.0))
    chips = max(wide // 2, 1)
    me_w = lax.axis_index("wide") if wide > 1 else 0
    me_n = lax.axis_index("narrow") if narrow > 1 else 0
    chip, core = (me_w // 2, lax.rem(me_w, 2)) if wide > 1 else (0, 0)
    shifts = Shifts(at["masks"], TILE)

    def block(index):
        return pl.ds(pl.multiple_of(index * share, share), share)

    def tile_at(t):
        return pl.ds(pl.multiple_of(t * TILE, TILE), TILE)

    def ahead(size, me, d):
        return lax.rem(me + d, size)

    def behind(size, me, d):
        return lax.rem(me + size - d, size)

    def each(first, size, fn):
        if wide > 1 and size > first:
            lax.fori_loop(first, size, lambda d, c: (fn(d), c)[1], 0)

    def remote(src, dst, sems, index, device):
        send, recv = at[sems + "_send"], at[sems + "_recv"]
        return pltpu.make_async_remote_copy(
            src_ref=src,
            dst_ref=dst,
            send_sem=send.at[index],
            recv_sem=recv.at[index],
            device_id=device,
            device_id_type=MESH,
        )

    class Exchange:
        def __init__(self, name):
            self.name, self.bufs = name, (at[name + "_w"], at[name + "_n"])

        def copy(self, phase, d, coming):
            axis, size, me = (("wide", wide, me_w), ("narrow", narrow, me_n))[phase]
            row = self.bufs[phase].at[behind(size, me, d) if coming else me]
            sems = self.name + ("_sw", "_sn")[phase]
            return remote(row, row, sems, d, {axis: ahead(size, me, d)})

        def start(self, phase, value):
            me, size = ((me_w, wide), (me_n, narrow))[phase]
            self.bufs[phase][me] = value
            each(1, size, lambda d: self.copy(phase, d, False).start())

        def finish(self, phase):
            size = (wide, narrow)[phase]

            def one(d):
                self.copy(phase, d, False).wait_send()
                self.copy(phase, d, True).wait_recv()

            each(1, size, one)
            value = self.bufs[phase][0]
            for k in range(1, size):
                value = value + self.bufs[phase][k]
            return value

        def hop(self):
            self.start(1, self.finish(0))

    stat, early, late = Exchange("stat"), Exchange("early"), Exchange("late")

    class Group:
        def __init__(self, name):
            self.name = name
            self.full, self.pair, self.chip = at[name], at[name + "_p"], at[name + "_c"]
            self.part, self.out = at[name + "_n"], at[name + "_out"]
            self.scatter = share % (8 * narrow) == 0
            self.piece = share // narrow if self.scatter else share
            self.stage = 0

        def rows(self, index):
            return pl.ds(pl.multiple_of(index * self.piece, 8), self.piece)

        def copies(self, stage):
            if stage == 0:
                go = lambda d: remote(
                    self.full.at[block(2 * d + 1 - core)],
                    self.pair.at[d],
                    self.name + "_s0",
                    d,
                    {"wide": me_w + 1 - 2 * core},
                )
                return 0, chips, go, go
            if stage == 1:

                def go(d):
                    to = 2 * ahead(chips, chip, d) + core
                    return remote(
                        self.full.at[block(to)], self.chip.at[d], self.name + "_s1", d, {"wide": to}
                    )

                return 1, chips, go, go
            if stage == 2 and self.scatter:

                def go(d):
                    to = ahead(narrow, me_n, d)
                    mine = pl.ds(pl.multiple_of(me_w * share + to * self.piece, 8), self.piece)
                    return remote(
                        self.full.at[mine], self.part.at[d], self.name + "_s2", d, {"narrow": to}
                    )

                return 1, narrow, go, go
            if stage == 2:
                go = lambda d: remote(
                    self.part.at[me_n],
                    self.part.at[me_n],
                    self.name + "_s2",
                    d,
                    {"narrow": ahead(narrow, me_n, d)},
                )
                come = lambda d: remote(
                    self.part.at[behind(narrow, me_n, d)],
                    self.part.at[behind(narrow, me_n, d)],
                    self.name + "_s2",
                    d,
                    {"narrow": ahead(narrow, me_n, d)},
                )
                return 1, narrow, go, come
            go = lambda d: remote(
                self.out.at[self.rows(me_n)],
                self.out.at[self.rows(me_n)],
                self.name + "_s3",
                d,
                {"narrow": ahead(narrow, me_n, d)},
            )
            come = lambda d: remote(
                self.out.at[self.rows(behind(narrow, me_n, d))],
                self.out.at[self.rows(behind(narrow, me_n, d))],
                self.name + "_s3",
                d,
                {"narrow": ahead(narrow, me_n, d)},
            )
            return 1, narrow if self.scatter else 1, go, come

        def start(self):
            first, end, go, _ = self.copies(self.stage)
            each(first, end, lambda d: go(d).start())

        def finish(self):
            first, end, go, come = self.copies(self.stage)

            def one(d):
                go(d).wait_send()
                come(d).wait_recv()

            each(first, end, one)
            own = block(me_w)
            if self.stage == 0:

                def add(d):
                    mine = block(2 * d + core)
                    self.full[mine, :] += self.pair[d]

                each(0, chips, add)
            if self.stage == 1:

                def add(d):
                    self.full[own, :] += self.chip[d]

                each(1, chips, add)
                if not self.scatter:
                    self.part[me_n] = self.full[own, :]
            if self.stage == 2 and self.scatter:
                mine = pl.ds(pl.multiple_of(me_w * share + me_n * self.piece, 8), self.piece)
                value = self.full[mine, :]
                for d in range(1, narrow):
                    value = value + self.part[d]
                self.out[self.rows(me_n), :] = value
            elif self.stage == 2:
                value = self.part[0]
                for d in range(1, narrow):
                    value = value + self.part[d]
                self.out[...] = value
            self.stage += 1

        def advance(self):
            if self.stage < 4:
                self.finish()
                if self.stage < 4:
                    self.start()

    made = {name: Group(name) for name in groups}

    if wide > 1:
        barrier = pltpu.get_barrier_semaphore()
        for axis, size, me in (("wide", wide, me_w), ("narrow", narrow, me_n)):
            each(
                1,
                size,
                lambda d: pl.semaphore_signal(
                    barrier, inc=1, device_id={axis: ahead(size, me, d)}, device_id_type=MESH
                ),
            )

    place = spread(164, SMALL).astype(bf16)
    for layer in range(layers):
        small_part = (
            dot(at["out"][layer].astype(bf16), place[0:108])
            + dot_tn(at["in"][:, layer, :].astype(bf16), place[108:162])
            + dot_tn(at["bias"][layer].astype(bf16), place[162:164])
        )
        wall[layer, block(me_w), 0:hid] = at["mid"][layer].astype(bf16)
        wall[layer, block(me_w), hid : hid + SMALL] = small_part.astype(bf16)

    def weights_of(index):
        return wall.at[0, block(index)]

    def to_chip(d, coming=False):
        index = 2 * (behind(chips, chip, d) if coming else chip) + core
        to = 2 * ahead(chips, chip, d) + core
        return remote(weights_of(index), weights_of(index), "ga", d, {"wide": to})

    def to_core(d, coming=False):
        index = 2 * behind(chips, chip, d) + (1 - core if coming else core)
        to = me_w + 1 - 2 * core
        return remote(weights_of(index), weights_of(index), "ga", chips + d, {"wide": to})

    def to_all(layer, d, coming=False):
        mine = wall.at[layer, block(behind(wide, me_w, d) if coming else me_w)]
        return remote(mine, mine, "gb", (layer, d), {"wide": ahead(wide, me_w, d)})

    if wide > 1:
        pl.semaphore_wait(barrier, wide + narrow - 2)
        each(1, chips, lambda d: to_chip(d).start())
        to_core(0).start()

    fill_masks(at["masks"])
    to_slots = spread_rows(16, 12)
    reverse = jnp.where(slot(11 - iota((16, 12), 1)) == iota((16, 12), 0), 1.0, 0.0)
    for layer in range(layers):
        small = at["small"][:, layer, :]
        lower, upper = mixing_parts(small[:, 0:12])
        scale = jnp.exp(small[:, 13:14])
        mixed = dot(reverse, dot(lower, upper, highest), highest) * as_row(scale)
        const = jnp.sum(mixed * as_row(small[:, 12:13]), axis=1, keepdims=True)
        cb = jnp.sum(to_slots * as_row(small[:, 14:15]), axis=1, keepdims=True)
        for c in range(12):
            mixes[layer, c] = jnp.broadcast_to(mixed[:, c : c + 1], (16, 128))
        mixes[layer, 12] = jnp.broadcast_to(const, (16, 128))
        mixes[layer, 13] = jnp.broadcast_to(cb, (16, 128))
        if layer:
            back = dot_nt(to_slots, mixed, highest)
            for c in range(12):
                s = c + 2 * (c // 6)
                mixes_back[layer, c] = jnp.broadcast_to(back[:, s : s + 1], (16, 128))

    def by_lanes(v):
        parts = [v[:, 128 * k : 128 * k + 128] for k in range(v.shape[1] // 128)]
        while len(parts) > 1:
            parts = [a + b for a, b in zip(parts[0::2], parts[1::2])]
        return parts[0]

    real = jnp.where(iota((8, 128), 0) < 6, 1.0, 0.0)

    def enter(layer, here, x):
        states[layer, :, here] = x
        y = wide_rows(mixes[layer, 12], TILE)
        for c in range(12):
            s = c + 2 * (c // 6)
            y = y + wide_rows(mixes[layer, c], TILE) * x[s : s + 1, :]
        ones = jnp.where(iota((8, TILE), 0) == 0, 1.0, 0.0)
        taps_in[layer, :, here] = jnp.concatenate(shifts.taps(y[0:8]) + [ones], axis=0).astype(bf16)
        states[layer + 1, 0:8, here] = y[0:8]
        keep[layer, 0:8, here] = y[8:16]

    def pixels_in(t, carry):
        images = TILE // 256
        blank = jnp.zeros((2, 256), f32)
        chunks = []
        for k in range(images):
            coarse = depth_ref[t * images + k] == 5
            by = jnp.where(coarse, 3, 0)
            level = jnp.where(coarse, 1.0 / 32.0, 1.0 / 256.0).astype(f32)
            at_image = pl.ds(pl.multiple_of(t * TILE + k * 256, 256), 256)
            quant = lax.shift_right_logical(pixels_ref[:, at_image], jnp.broadcast_to(by, (12, 256)))
            x = (quant.astype(f32) + noise_ref[:, at_image]) * level - 0.5
            chunks.append(jnp.concatenate([x[0:6], blank, x[6:12], blank], axis=0))
        enter(0, tile_at(t), jnp.concatenate(chunks, axis=1))
        return carry

    lax.fori_loop(0, count // TILE, pixels_in, 0)

    if wide > 1:

        def pass_on(d):
            to_chip(d).wait_send()
            to_chip(d, True).wait_recv()
            to_core(d).start()

        each(1, chips, pass_on)

    prior = at["prior"][...]
    s = iota((55, 256), 0)
    lane = iota((55, 256), 1)
    hit = (slot(s) == lane) | (slot(s) + 72 == lane) | (slot(s) + 144 == lane)
    to_taps = jnp.where(((s < 54) & hit) | ((s == 54) & (lane == 216)), 1.0, 0.0)
    prior_slots = dot(to_slots, prior, highest)
    parts = split_three(dot(prior_slots, to_taps, highest))
    at["prior_fwd"][...] = jnp.concatenate(parts, axis=0).astype(bf16)
    turned = dot_nt(spread_rows(72, 55), prior_slots, highest)
    stacked = jnp.concatenate(list(split_three(turned)) + [jnp.zeros((8, 16), f32)], axis=0)
    again = jnp.where((iota((16, 48), 1) & 15) == iota((16, 48), 0), 1.0, 0.0)
    at["prior_back"][...] = dot(stacked.astype(bf16), again.astype(bf16)).astype(bf16)

    for name in ("stat_acc", "like_acc", "prior_acc", "small_acc", "sum_acc", "bone_acc", "gst"):
        at[name][...] = jnp.zeros_like(at[name])
    for layer in range(layers):
        at[f"mid{layer}"][...] = jnp.zeros_like(at[f"mid{layer}"])

    pick = jnp.where(iota((SMALL, 128), 0) == iota((SMALL, 128), 1) + OUT, 1.0, 0.0).astype(bf16)

    def derive(layer):
        wsm = wall[layer, :, hid : hid + SMALL]
        win[layer] = dot(wsm, pick).astype(bf16)
        wst[layer] = wsm.T
        bone[layer] = jnp.broadcast_to(wsm[:, 217:218].astype(f32), (hid, 128))

    if wide > 1:

        def landed(d):
            to_core(d).wait_send()
            to_core(d, True).wait_recv()

        each(0, chips, landed)
        for layer in range(1, layers):
            each(1, wide, lambda d: to_all(layer, d).start())

    for layer in range(layers):
        if layer and wide > 1:

            def arrived(d):
                to_all(layer, d).wait_send()
                to_all(layer, d, True).wait_recv()

            each(1, wide, arrived)
        derive(layer)

        def forward(t, carry):
            here = tile_at(t)
            first = dot(win[layer, :, 0:80], taps_in[layer, :, here]).astype(bf16)
            h1 = jnp.maximum(first, jnp.zeros_like(first))
            hidden_one[layer, :, here] = h1
            second = dot(wall[layer, :, 0:hid], h1) + wide_rows(bone[layer], TILE)
            h2 = jnp.maximum(second, 0.0).astype(bf16)
            hidden_two[layer, :, here] = h2
            taps_out = dot(wst[layer, 0:OUT, :], h2)
            o = shifts.fold([taps_out[16 * k : 16 * k + 16] for k in range(9)])
            o = o + wide_rows(mixes[layer, 13], TILE)
            v = keep[layer, 0:8, here] + o[0:8]
            decay = 1.0 + jnp.exp(-(o[8:16] + 2.0))
            q = 1.0 / decay
            at["like_acc"][...] -= by_lanes(jnp.log(decay)) * real
            keep[layer, 0:8, here] = v
            keep[layer, 8:16, here] = q
            x = jnp.concatenate([states[layer + 1, 0:8, here], v * q], axis=0)
            if layer < layers - 1:
                enter(layer + 1, here, x)
            else:
                states[layer + 1, 8:16, here] = x[8:16]
                at["stat_acc"][0] += by_lanes(x)
                at["stat_acc"][1] += by_lanes(x * x)
            return carry

        lax.fori_loop(0, count // TILE, forward, 0)

    lane = iota((16, 128), 1)

    def columns(*parts):
        value = jnp.zeros((16, 128), f32)
        for k, part in enumerate(parts):
            value = jnp.where(lane == k, jnp.sum(part, axis=1, keepdims=True), value)
        return value

    stat.start(0, columns(at["stat_acc"][0], at["stat_acc"][1]))

    def prior_tile(t, carry):
        here = tile_at(t)
        z1 = states[layers, 0:8, here]
        z2 = states[layers, 8:16, here]
        ones = jnp.where(iota((8, TILE), 0) == 0, 1.0, 0.0)
        pieces = [split_three(v) for v in shifts.taps(z1)]
        tz = jnp.concatenate(
            [p[0] for p in pieces] + [p[1] for p in pieces] + [p[2] for p in pieces] + [ones], axis=0
        ).astype(bf16)
        three = dot(at["prior_fwd"][:, 0:224], tz)
        value = three[0:16] + three[16:32] + three[32:48]
        centre, log_sd = value[0:8], value[8:16]
        inverse = jnp.exp(-log_sd)
        ratio = (z2 - centre) * inverse
        at["like_acc"][...] += by_lanes(-0.5 * z1 * z1 - 0.5 * ratio * ratio - log_sd)
        d_centre = ratio * inverse
        d_stat = jnp.concatenate([d_centre, ratio * ratio - 1.0], axis=0)
        ds = jnp.concatenate(split_three(d_stat), axis=0).astype(bf16)
        at["prior_acc"][:, 0:224] += dot_nt(ds, tz)
        dt = dot(at["prior_back"][...], ds)
        dt = dt[0:72] + dt[72:144] + dt[144:216]
        folded = shifts.fold([dt[8 * k : 8 * k + 8] for k in range(9)], -1)
        gz[0:8, here] = coeff * (folded - z1)
        gz[8:16, here] = -coeff * d_centre
        return carry

    tiles = count // TILE
    lax.fori_loop(0, tiles // 2, prior_tile, 0)
    stat.hop()
    lax.fori_loop(tiles // 2, tiles, prior_tile, 0)
    for layer in range(layers):
        wmt[layer] = wall[layer, :, 0:hid].T
    stats = stat.finish(1)
    mean = stats[:, 0:1] / total
    var = stats[:, 1:2] / total - mean * mean
    from_first = penalty_weight * (2.0 * mean - 4.0 * (var - 1.0) * mean) / total
    from_square = penalty_weight * 2.0 * (var - 1.0) / total
    ones_rows = jnp.where((iota((16, 1), 0) & 7) < 6, 1.0, 0.0)
    penalty = penalty_weight * jnp.sum(
        ones_rows * (mean * mean + (var - 1.0) * (var - 1.0)), axis=0, keepdims=True
    )

    def back_a(layer, t, carry):
        here = tile_at(t)
        g = gz[:, here]
        if layer == layers - 1:
            g = g + from_first + 2.0 * states[layers, :, here] * from_square
            gz[0:8, here] = g[0:8]
        v = keep[layer, 0:8, here]
        q = keep[layer, 8:16, here]
        gbq = g[8:16] * q
        gz[8:16, here] = gbq
        do = jnp.concatenate([gbq, (gbq * v + coeff) * (1.0 - q)], axis=0)
        at["sum_acc"][layer, 1] += by_lanes(do)
        rounded = do.astype(bf16).astype(f32)
        d3 = jnp.concatenate(shifts.taps(rounded, -1), axis=0).astype(bf16)
        h2 = hidden_two[layer, :, here]
        at["gst"][0:OUT, :] += dot_nt(d3, h2)
        dd2 = dot(wall[layer, :, hid : hid + OUT], d3).astype(bf16)
        hidden_two[layer, :, here] = jnp.where(h2 > 0, dd2, jnp.zeros_like(dd2))
        return carry

    def back_b(layer, t, carry):
        here = tile_at(t)
        d2 = hidden_two[layer, :, here]
        at[f"mid{layer}"][...] += dot_nt(d2, hidden_one[layer, :, here])
        at["bone_acc"][...] += by_lanes(d2.astype(f32))
        return carry

    def back_c(layer, t, carry):
        here = tile_at(t)
        dd1 = dot(wmt[layer], hidden_two[layer, :, here]).astype(bf16)
        d1 = jnp.where(hidden_one[layer, :, here] > 0, dd1, jnp.zeros_like(dd1))
        at["gst"][OUT : OUT + 80, :] += dot_nt(taps_in[layer, :, here], d1)
        dt = dot(wst[layer, OUT : OUT + 80, :], d1)
        g = gz[:, here]
        gya = g[0:8] + shifts.fold([dt[8 * k : 8 * k + 8] for k in range(9)], -1)
        gy = jnp.concatenate([gya, g[8:16]], axis=0)
        at["sum_acc"][layer, 0] += by_lanes(gy)
        left = jnp.concatenate(split_three(gy), axis=0).astype(bf16)
        right = jnp.concatenate(split_three(states[layer, :, here]), axis=0).astype(bf16)
        at["small_acc"][layer, :, 0:48] += dot_nt(left, right)
        if layer:
            gx = wide_rows(mixes_back[layer, 0], TILE) * gy[0:1, :]
            for c in range(1, 12):
                s = c + 2 * (c // 6)
                gx = gx + wide_rows(mixes_back[layer, c], TILE) * gy[s : s + 1, :]
            gz[:, here] = gx
        return carry

    def moments(layer):
        acc = at["small_acc"][layer]
        part = acc[0:16] + acc[16:32] + acc[32:48]
        moment = part + pltpu.roll(part, 112, 1) + pltpu.roll(part, 96, 1)
        moment = jnp.where(lane < 16, moment, 0.0)
        for k in range(2):
            line = jnp.sum(at["sum_acc"][layer, k], axis=1, keepdims=True)
            moment = moment + jnp.where(lane == 16 + k, line, 0.0)
        return moment

    def early_sums():
        acc = at["prior_acc"][0:16] + at["prior_acc"][16:32] + at["prior_acc"][32:48]
        last = pltpu.roll(acc, 256 - 144, 1)
        taps_part = (acc + pltpu.roll(acc, 256 - 72, 1) + last)[:, 0:128]
        pieces = [moments(layer) for layer in range(1, layers)]
        pieces.append(
            jnp.where(lane < 72, taps_part, 0.0) + jnp.where(lane == 72, last[:, 0:128], 0.0)
        )
        depths = lax.fori_loop(0, depth_ref.shape[0], lambda k, c: c + depth_ref[k], jnp.int32(0))
        depths = jnp.broadcast_to(depths, (8, 128)).astype(f32)
        row8 = iota((8, 128), 0)
        logs = jnp.sum(at["like_acc"][...], axis=0, keepdims=True)
        pieces.append(jnp.where(row8 == 0, logs, 0.0) + jnp.where(row8 == 1, depths, 0.0))
        return jnp.concatenate(pieces, axis=0)

    running = []

    def advance_all():
        for group in running:
            group.advance()

    def launch(name):
        made[name].start()
        running.append(made[name])

    half = tiles // 2
    for layer in reversed(range(layers)):
        lax.fori_loop(0, tiles, functools.partial(back_a, layer), 0)
        at[f"out{layer}"][...] = at["gst"][0:128, :].T
        advance_all()
        launch(f"out{layer}")
        if not layer:
            early.hop()
        lax.fori_loop(0, tiles, functools.partial(back_b, layer), 0)
        advance_all()
        launch(f"mid{layer}")
        if not layer:
            early_total = early.finish(1)
        lax.fori_loop(0, half, functools.partial(back_c, layer), 0)
        advance_all()
        lax.fori_loop(half, tiles, functools.partial(back_c, layer), 0)
        column = jnp.sum(at["bone_acc"][...], axis=1, keepdims=True)
        at[f"inn{layer}"][...] = jnp.where(
            iota((hid, 128), 1) == 217 - 128, column, at["gst"][128:SMALL, :].T
        )
        if layer:
            advance_all()
            launch(f"inn{layer}")
            at["gst"][...] = jnp.zeros_like(at["gst"])
            at["bone_acc"][...] = jnp.zeros_like(at["bone_acc"])
            if layer == 1:
                early.start(0, early_sums())
        else:
            late.start(0, moments(0))
            launch("inn0")
    advance_all()
    late.hop()
    while any(group.stage < 4 for group in running):
        advance_all()
    late_total = late.finish(1)
    for layer in range(layers):
        at["grad"][layer, :, 0:hid] = made[f"mid{layer}"].out[...]
        at["grad"][layer, :, hid : hid + 128] = made[f"out{layer}"].out[...]
        at["grad"][layer, :, hid + 128 : hid + SMALL] = made[f"inn{layer}"].out[...]
    whole = jnp.concatenate([late_total, early_total], axis=0)
    rows = whole.shape[0]
    at["sums"][...] = whole + jnp.where(iota((rows, 128), 0) == rows - 8 + 2, penalty, 0.0)


def adamw(weight, grad, first, second, fixes):
    first_new = beta_one * first + (1.0 - beta_one) * grad
    second_new = beta_two * second + (1.0 - beta_two) * grad * grad
    update = first_new / fixes[0] / (jnp.sqrt(second_new / fixes[1]) + epsilon) + decay_rate * weight
    return (weight - learn_rate * update, first_new, second_new)


def update_kernel(total, images, step_ref, grad_ref, sums_ref, *refs):
    weights, firsts, seconds, loss_ref, outs = refs[0:6], refs[6:12], refs[12:18], refs[18], refs[19:]
    layers, share, _ = grad_ref.shape
    hid = weights[1].shape[2]
    coeff = -1.0 / (total * 12 * math.log(2.0))
    power = iota((8, 128), 1)
    used = power < jnp.broadcast_to(step_ref[0], (8, 128))
    fixes = tuple(
        (1.0 - beta)
        * jnp.sum(
            jnp.where(used, jnp.exp(power.astype(f32) * math.log(beta)), 0.0), axis=1, keepdims=True
        )[0:1]
        for beta in (beta_one, beta_two)
    )

    def write(which, at, grad):
        new = adamw(weights[which][at], grad, firsts[which][at], seconds[which][at], fixes)
        for k in range(3):
            outs[3 * which + k][at] = new[k]

    def column(layer):
        return (slice(None), layer, slice(None))

    place = spread(164, SMALL)
    to_slots = spread_rows(16, 12)
    reverse = jnp.where(slot(11 - iota((16, 12), 1)) == iota((16, 12), 0), 1.0, 0.0)
    row, col = iota((12, 12), 0), iota((12, 12), 1)
    eye = row == col
    logdet = jnp.zeros((1, 1), f32)
    for layer in range(layers):
        write(1, layer, grad_ref[layer, :, 0:hid])
        part = grad_ref[layer, :, hid : hid + SMALL]
        write(0, column(layer), dot_nt(place[108:162], part, highest))
        write(2, layer, dot_nt(part, place[0:108], highest))
        write(3, layer, dot_nt(place[162:164], part, highest))
        small = weights[4][column(layer)]
        lu = small[:, 0:12]
        lower, upper = mixing_parts(lu)
        scale = jnp.exp(small[:, 13:14])
        scale_row = as_row(scale)
        sums = sums_ref[16 * layer : 16 * layer + 16]
        turned = dot_tn(reverse, sums, highest)
        moment = dot(turned[:, 0:16], to_slots, highest)
        ones = turned[:, 16:17]
        g_mix = (moment + ones * as_row(small[:, 12:13])) * scale_row
        mix = dot(lower, upper, highest)
        g_bias = scale * dot_tn(mix, ones, highest)
        g_scale = as_column(jnp.sum(mix * g_mix, axis=0, keepdims=True)) + coeff * total
        g_lower = dot_nt(g_mix, upper, highest)
        g_upper = dot_tn(lower, g_mix, highest)
        g_lu = jnp.where(row > col, g_lower, jnp.where(eye, g_upper * jnp.exp(lu) + coeff * total, g_upper))
        g_cb = dot_tn(to_slots, sums, highest)[:, 17:18]
        wide15 = iota((12, 15), 1)
        grad = dot(g_lu, jnp.where(iota((12, 15), 0) == wide15, 1.0, 0.0), highest)
        grad = jnp.where(wide15 == 12, g_bias, grad)
        grad = jnp.where(wide15 == 13, g_scale, grad)
        grad = jnp.where(wide15 == 14, g_cb, grad)
        write(4, column(layer), grad)
        diag = jnp.sum(jnp.where(eye, lu, 0.0), axis=0, keepdims=True) + as_row(small[:, 13:14])
        logdet = logdet + jnp.sum(diag, axis=1, keepdims=True)
    sums = sums_ref[16 * layers : 16 * layers + 16]
    grad = coeff * dot_nt(
        dot_tn(to_slots, sums, highest), spread(55, 128), highest
    )
    write(5, Ellipsis, grad)
    tail = sums_ref[16 * layers + 16 :]
    likely = jnp.sum(tail[0:1], axis=1, keepdims=True)
    likely = likely - total * 6.0 * math.log(2.0 * math.pi) + total * logdet
    loss_ref[...] = coeff * likely + tail[1:2, 0:1] / images + tail[2:3, 0:1]


def as_column(row):
    n = row.shape[1]
    eye = iota((n, n), 0) == iota((n, n), 1)
    return jnp.sum(jnp.where(eye, row, 0.0), axis=1, keepdims=True)


def turn(arrays, back=False):
    orders = ((1, 2, 0) if back else (2, 0, 1), None, (0, 2, 1), None, (1, 0, 2), None)
    return tuple(a if o is None else jnp.transpose(a, o) for a, o in zip(arrays, orders))


def shards(*args, wide, narrow):
    pixels, noise, depth, step_count = args[0:4]
    params, firsts, seconds = turn(args[4:10]), turn(args[10:16]), turn(args[16:22])
    layers, share, hid = params[1].shape
    count = pixels.shape[1]
    chips = max(wide // 2, 1)
    width = hid + SMALL
    early = 16 * layers + 8
    rows = early + 16
    dma = pltpu.SemaphoreType.DMA
    names = ["pixels", "noise", "depth", "small", "prior", "in", "mid", "out", "bias", "grad", "sums"]
    scratch = []

    def add(name, kind):
        names.append(name)
        scratch.append(kind)

    def sems(name, shape):
        add(name + "_send", dma(shape))
        add(name + "_recv", dma(shape))

    for name, shape, dtype in (
        ("wall", (layers, hid, width), bf16),
        ("wmt", (layers, hid, hid), bf16),
        ("wst", (layers, SMALL, hid), bf16),
        ("win", (layers, hid, 128), bf16),
        ("bone", (layers, hid, 128), f32),
        ("mixes", (layers, 14, 16, 128), f32),
        ("mixes_back", (layers, 12, 16, 128), f32),
        ("prior_fwd", (48, 256), bf16),
        ("prior_back", (224, 48), bf16),
        ("masks", (4, 8, TILE), f32),
        ("states", (layers + 1, 16, count), f32),
        ("keep", (layers, 16, count), f32),
        ("taps_in", (layers, 80, count), bf16),
        ("hidden_one", (layers, hid, count), bf16),
        ("hidden_two", (layers, hid, count), bf16),
        ("gz", (16, count), f32),
        ("stat_acc", (2, 16, 128), f32),
        ("like_acc", (8, 128), f32),
        ("prior_acc", (48, 256), f32),
        ("small_acc", (layers, 48, 128), f32),
        ("sum_acc", (layers, 2, 16, 128), f32),
        ("bone_acc", (hid, 128), f32),
        ("gst", (SMALL, hid), f32),
    ):
        add(name, pltpu.VMEM(shape, dtype))
    for name, height in (("stat", 16), ("early", early), ("late", 16)):
        add(name + "_w", pltpu.VMEM((wide, height, 128), f32))
        add(name + "_n", pltpu.VMEM((narrow, height, 128), f32))
        sems(name + "_sw", (wide,))
        sems(name + "_sn", (narrow,))
    groups = []
    piece = share // narrow if share % (8 * narrow) == 0 else share
    for layer in range(layers):
        for kind, across in (("mid", hid), ("out", 128), ("inn", 128)):
            name = f"{kind}{layer}"
            groups.append(name)
            add(name, pltpu.VMEM((hid, across), f32))
            add(name + "_p", pltpu.VMEM((chips, share, across), f32))
            add(name + "_c", pltpu.VMEM((chips, share, across), f32))
            add(name + "_n", pltpu.VMEM((narrow, piece, across), f32))
            add(name + "_out", pltpu.VMEM((share, across), f32))
            for stage, size in enumerate((chips, chips, narrow, narrow)):
                sems(f"{name}_s{stage}", (size,))
    sems("ga", (2 * chips,))
    sems("gb", (layers, wide))
    remote = {"collective_id": 0, "has_side_effects": True} if wide > 1 else {}
    grads, sums = pl.pallas_call(
        functools.partial(flow_kernel, wide, narrow, (names, groups)),
        out_shape=(
            jax.ShapeDtypeStruct((layers, share, width), f32),
            jax.ShapeDtypeStruct((rows, 128), f32),
        ),
        in_specs=[VMEM, VMEM, SMEM] + [VMEM] * 6,
        out_specs=(VMEM, VMEM),
        scratch_shapes=scratch,
        compiler_params=pltpu.CompilerParams(vmem_limit_bytes=FLOW_VMEM, **remote),
        name="flow",
    )(pixels, noise, depth, params[4], params[5], *params[0:4])
    total = count * wide * narrow
    shapes = [jax.ShapeDtypeStruct((1, 1), f32)]
    for p in params:
        shapes += [jax.ShapeDtypeStruct(p.shape, f32)] * 3
    results = pl.pallas_call(
        functools.partial(update_kernel, total, total // 256),
        out_shape=tuple(shapes),
        in_specs=[SMEM] + [VMEM] * 20,
        out_specs=(VMEM,) * 19,
        compiler_params=pltpu.CompilerParams(vmem_limit_bytes=UPDATE_VMEM),
        name="update",
    )(step_count.reshape(1), grads, sums, *params, *firsts, *seconds)
    updated = [turn(results[1 + k :: 3], True) for k in range(3)]
    return (results[0].reshape(()),) + tuple(updated[k][p] for p in range(6) for k in range(3))


def solution(mesh):
    weights = (P(None, "wide", None), P(None, "wide", None), P(None, None, "wide"), P(None, None, "wide"), P(), P())
    return jax.shard_map(
        functools.partial(shards, wide=mesh.shape["wide"], narrow=mesh.shape["narrow"]),
        mesh=mesh,
        in_specs=(
            P(None, ("narrow", "wide")),
            P(None, ("narrow", "wide")),
            P(("narrow", "wide")),
            P(),
        )
        + weights * 3,
        out_specs=(P(),) + tuple(w for w in weights for _ in range(3)),
        check_vma=False,
    )
```

time: 225 us -> 114 us (0.51)
  Pallas kernels: 200 us -> 112 us
  local copies, waits for them, and re-layouts: 21.6 us -> 0 us
    pallas_call x1, Pallas kernels: 197 us -> 108 us  [shards(): pl.pallas_call(functools.partial(flow_kernel, wide, narrow, (names, group...]
    unnamed x62 -> x0, local copies, waits for them, and re-layouts: 21.6 us -> none
where the time goes in v2:
time: 114 us
  Pallas kernels  112 us (98%)
  between operations  1.47 us (1%)
    pallas_call x1, Pallas kernels, shards(): pl.pallas_call(functools.partial(flow_kernel, wide, narrow, (names, group...  108 us
    pallas_call x1, Pallas kernels, shards(): pl.pallas_call(functools.partial(update_kernel, total, total // 256), out...  4.09 us

profile of v2, /device:TPU:0, one launch (start us, length us, event | category | flops | bytes accessed | tf_op | source)
XLA Modules:
  0.0 113.9 jit_solution(17200501831908114685)
XLA Ops:
  1.3 108.3 %flow.1 = (f32[2,64,768]{2,1,0:T(8,128)}, f32[56,128]{1,0:T(8,128)}) custom-call(s32[12,8192]{1,0:T(8,128)} %refs_0_.1, f32[12,8192]{1,0:T(8,128)} %refs_1_.2, s32[32]{0:T(128)} %refs_2_.1, f32[12,2,15]{2,1,0:T(2,128)} %bitcast.29, f32[12,55]{1,0:T(8,128)} %refs_5_.1, f32[54,2,64]{2,1,0:T(2,128)} %bitcast.23, f32[2,64,512]{2,1,0:T(8,128)} %refs_1_.3, ...), custom_call_target="tpu_custom_call" | custom-call | tf_op jit(solution)/shard_map/flow/pallas_call | solution.py:853
  109.6 4.1 %update.1 = (f32[1,1]{1,0:T(1,128)}, f32[54,2,64]{2,1,0:T(2,128)}, f32[54,2,64]{2,1,0:T(2,128)}, f32[54,2,64]{2,1,0:T(2,128)}, f32[2,64,512]{2,1,0:T(8,128)}, /*...) custom-call(s32[1]{0:T(128)} %bitcast.20.step_ref, ...), custom_call_target="tpu_custom_call" | custom-call | tf_op jit(solution)/shard_map/update/pallas_call | solution.py:869

commit v3 on v2

v3 whole, which is shorter than its diff:
```python
import functools
import math
from types import SimpleNamespace

import jax
import jax.numpy as jnp
from jax import lax
from jax.experimental import pallas as pl
from jax.experimental.pallas import tpu as pltpu
from jax.sharding import PartitionSpec as P

f32 = jnp.float32
bf16 = jnp.bfloat16
highest = lax.Precision.HIGHEST
MESH = pl.DeviceIdType.MESH
learn_rate = 0.02
beta_one = 0.9
beta_two = 0.999
epsilon = 1e-08
decay_rate = 0.01
penalty_weight = 0.5
tap_offsets = [(r, c) for r in (-1, 0, 1) for c in (-1, 0, 1)]
TILE = 2048
FLOW_VMEM = 62 * 1024 * 1024
UPDATE_VMEM = 60 * 1024 * 1024
OUT = 144
SMALL = 256
VMEM = pl.BlockSpec(memory_space=pltpu.VMEM)
SMEM = pl.BlockSpec(memory_space=pltpu.SMEM)
HBM = pl.BlockSpec(memory_space=pl.ANY)
WIDE, NARROW = "wide", "narrow"


def dot(a, b, precision=None):
    return lax.dot_general(
        a, b, (((1,), (0,)), ((), ())), preferred_element_type=f32, precision=precision
    )


def dot_nt(a, b, precision=None):
    return lax.dot_general(
        a, b, (((1,), (1,)), ((), ())), preferred_element_type=f32, precision=precision
    )


def dot_tn(a, b, precision=None):
    return lax.dot_general(
        a, b, (((0,), (0,)), ((), ())), preferred_element_type=f32, precision=precision
    )


def iota(shape, axis):
    return lax.broadcasted_iota(jnp.int32, shape, axis)


def slot(s):
    return s + 2 * ((s * 10923) >> 16)


def spread(count, width, first=0):
    return jnp.where(slot(iota((count, width), 0) + first) == iota((count, width), 1), 1.0, 0.0)


def spread_rows(height, count):
    return jnp.where(slot(iota((height, count), 1)) == iota((height, count), 0), 1.0, 0.0)


def split_two(v):
    high = v.astype(bf16).astype(f32)
    return high, v - high


def as_row(column):
    n = column.shape[0]
    eye = iota((n, n), 0) == iota((n, n), 1)
    return jnp.sum(jnp.where(eye, column, 0.0), axis=0, keepdims=True)


def as_column(row):
    n = row.shape[1]
    eye = iota((n, n), 0) == iota((n, n), 1)
    return jnp.sum(jnp.where(eye, row, 0.0), axis=1, keepdims=True)


def mixing_parts(lu):
    n = lu.shape[0]
    row, col = iota((n, n), 0), iota((n, n), 1)
    lower = jnp.where(row > col, lu, 0.0) + jnp.where(row == col, 1.0, 0.0)
    upper = jnp.where(row < col, lu, 0.0) + jnp.where(row == col, jnp.exp(lu), 0.0)
    return lower, upper


def wide_rows(v, lanes):
    return jnp.concatenate([v] * (lanes // 128), axis=1)


class Shifts:
    def __init__(self, mask_ref, lanes):
        self.lanes = lanes
        self.masks = mask_ref

    def mask(self, which, rows):
        m = self.masks[which, :, 0 : self.lanes]
        return jnp.concatenate([m] * (rows // 8), axis=0) if rows > 8 else m

    def col(self, v, c):
        if c == 0:
            return v
        moved = pltpu.roll(v, (-c) % self.lanes, 1)
        return moved * self.mask(0 if c > 0 else 1, v.shape[0])

    def row(self, v, r):
        if r == 0:
            return v
        moved = pltpu.roll(v, (-16 * r) % self.lanes, 1)
        return moved * self.mask(2 if r > 0 else 3, v.shape[0])

    def taps(self, v, sign=1):
        by_col = {c: self.col(v, c) for c in (-1, 0, 1)}
        return [self.row(by_col[sign * c], sign * r) for r, c in tap_offsets]

    def fold(self, pieces, sign=1):
        total = None
        for c in (-1, 0, 1):
            part = None
            for r in (-1, 0, 1):
                piece = self.row(pieces[3 * (r + 1) + (c + 1)], sign * r)
                part = piece if part is None else part + piece
            part = self.col(part, sign * c)
            total = part if total is None else total + part
        return total


def fill_masks(mask_ref):
    lanes = mask_ref.shape[2]
    pos = iota((8, lanes), 1)
    row, col = (pos >> 4) & 15, pos & 15
    for which, keep in enumerate((col < 15, col > 0, row < 15, row > 0)):
        mask_ref[which] = jnp.where(keep, 1.0, 0.0)


def flow_kernel(wide, narrow, tree, *refs):
    hbm, grads, at = (SimpleNamespace(**part) for part in jax.tree.unflatten(tree, refs))
    wmid, wsmall, wmt, wst, win = at.wmid, at.wsmall, at.wmt, at.wst, at.win
    bone, mixes, mixes_back = at.bone, at.mixes, at.mixes_back
    gz, gy_ref, d3, tbuf = at.gz, at.gy, at.d3, at.tbuf
    given = SimpleNamespace(**at.given)
    layers, share, hid = given.mid.shape
    count = given.pixels.shape[1]
    total = count * wide * narrow
    coeff = -1.0 / (total * 12 * math.log(2.0))
    chips = max(wide // 2, 1)
    me_w = lax.axis_index(WIDE) if wide > 1 else 0
    me_n = lax.axis_index(NARROW) if narrow > 1 else 0
    chip, core = (me_w // 2, lax.rem(me_w, 2)) if wide > 1 else (0, 0)
    shifts = Shifts(at.masks, TILE)

    def block(index):
        return pl.ds(pl.multiple_of(index * share, share), share)

    def tile_at(t):
        return pl.ds(pl.multiple_of(t * TILE, TILE), TILE)

    def ahead(size, me, d):
        return lax.rem(me + d, size)

    def behind(size, me, d):
        return lax.rem(me + size - d, size)

    def each(first, size, fn):
        if wide > 1 and size > first:
            lax.fori_loop(first, size, lambda d, c: (fn(d), c)[1], 0)

    def remote(src, dst, sems, index, device):
        return pltpu.make_async_remote_copy(
            src_ref=src,
            dst_ref=dst,
            send_sem=sems[0].at[index],
            recv_sem=sems[1].at[index],
            device_id=device,
            device_id_type=MESH,
        )

    def drain(ref, sem):
        if wide > 1:
            pltpu.make_async_copy(ref, ref, sem.at[0]).wait()

    class Exchange:
        def __init__(self, bufs, sems):
            self.bufs, self.sems = bufs, sems

        def copy(self, phase, d):
            axis, size, me = ((WIDE, wide, me_w), (NARROW, narrow, me_n))[phase]
            row = self.bufs[phase].at[me]
            return remote(row, row, self.sems[phase], 0, {axis: ahead(size, me, d)})

        def start(self, phase, value):
            me, size = ((me_w, wide), (me_n, narrow))[phase]
            self.bufs[phase][me] = value
            each(1, size, lambda d: self.copy(phase, d).start())

        def finish(self, phase):
            size = (wide, narrow)[phase]
            if size > 1:
                for sem in self.sems[phase]:
                    drain(self.bufs[phase].at[1:size], sem)
            value = self.bufs[phase][0]
            for k in range(1, size):
                value = value + self.bufs[phase][k]
            return value

        def hop(self):
            self.start(1, self.finish(0))

    class OneShot:
        def __init__(self, rows, sems):
            self.rows, self.sems = rows, sems

        def copy(self, d):
            by_n, by_w = d // wide, lax.rem(d, wide)
            row = self.rows.at[me_n * wide + me_w]
            device = {NARROW: ahead(narrow, me_n, by_n), WIDE: ahead(wide, me_w, by_w)}
            return remote(row, row, self.sems, 0, device)

        def start(self, value):
            self.rows[me_n * wide + me_w] = value
            each(1, wide * narrow, lambda d: self.copy(d).start())

        def finish(self):
            if wide > 1:
                for sem in self.sems:
                    drain(self.rows.at[1 : wide * narrow], sem)
            return lax.fori_loop(
                0, wide * narrow, lambda k, c: c + self.rows[k], jnp.zeros(self.rows.shape[1:], f32)
            )

    stat, late = OneShot(*at.stat), OneShot(*at.late)
    early = Exchange(*at.early)

    class Group:
        def __init__(self, refs):
            self.full, self.pair, self.chip, self.part, self.out = refs[0:5]
            self.sems = refs[5]
            self.piece = self.part.shape[1]
            self.scatter = self.piece < share
            self.stage = 0
            self.last = 3 if self.scatter else 2

        def mine(self, index):
            return pl.ds(pl.multiple_of(index * self.piece, 8), self.piece)

        def start(self):
            sems = self.sems[self.stage]
            if self.stage == 0:
                if wide > 1:
                    theirs = self.full.at[:, 1 - core]
                    remote(theirs, self.pair, sems, 0, {WIDE: me_w + 1 - 2 * core}).start()
                return

            def go(d):
                if self.stage == 1:
                    to = ahead(chips, chip, d)
                    remote(self.full.at[to, core], self.chip.at[d - 1], sems, 0, {WIDE: 2 * to + core}).start()
                    return
                to = ahead(narrow, me_n, d)
                if self.stage == 2 and self.scatter:
                    rows = self.full.at[chip, core, self.mine(to)]
                    remote(rows, self.part.at[d - 1], sems, 0, {NARROW: to}).start()
                    return
                ref = self.part.at[me_n] if self.stage == 2 else self.out.at[self.mine(me_n)]
                remote(ref, ref, sems, 0, {NARROW: to}).start()

            each(1, chips if self.stage == 1 else narrow, go)

        def finish(self):
            if self.stage == 0:
                come = self.pair
            elif self.stage == 1:
                come = self.chip.at[0 : chips - 1] if chips > 1 else None
            elif self.stage == 2:
                come = self.part.at[0 : narrow - 1] if narrow > 1 else None
            else:
                come = self.out.at[0 : (narrow - 1) * self.piece] if narrow > 1 else None
            if come is not None:
                for sem in self.sems[self.stage]:
                    drain(come, sem)
            own = (chip, core)
            if self.stage == 0:

                def add(d):
                    self.full[d, core] += self.pair[d]

                each(0, chips, add)
            if self.stage == 1:
                value = self.full[own]
                for d in range(chips - 1):
                    value = value + self.chip[d]
                if self.scatter:
                    self.full[own] = value
                else:
                    self.part[me_n] = value
            if self.stage == 2:
                value = self.full[chip, core, self.mine(me_n)] if self.scatter else self.part[0]
                for d in range(0 if self.scatter else 1, narrow - 1 if self.scatter else narrow):
                    value = value + self.part[d]
                self.out[self.mine(me_n) if self.scatter else slice(None)] = value
            self.stage += 1

        def put(self, value):
            self.full[...] = value.reshape(self.full.shape)

        def add(self, value):
            self.full[...] += value.reshape(self.full.shape)

        def advance(self):
            self.finish()
            if self.stage <= self.last:
                self.start()

    mid, out, inn = ([Group(refs) for refs in kind] for kind in (at.mid, at.out, at.inn))

    if wide > 1:
        barrier = pltpu.get_barrier_semaphore()
        each(
            1,
            wide * narrow,
            lambda d: pl.semaphore_signal(
                barrier,
                inc=1,
                device_id={
                    NARROW: ahead(narrow, me_n, d // wide),
                    WIDE: ahead(wide, me_w, lax.rem(d, wide)),
                },
                device_id_type=MESH,
            ),
        )
    loads = {
        name: pltpu.make_async_copy(source_ref, at.given[name], at.load.at[k])
        for k, (name, source_ref) in enumerate(vars(hbm).items())
    }
    for copy in loads.values():
        copy.start()
    loads = SimpleNamespace(**loads)

    place = spread(164, SMALL).astype(bf16)
    for copy in (loads.mid, loads.first, loads.out, loads.bias):
        copy.wait()
    for layer in range(layers):
        small_part = (
            dot(given.out[layer].astype(bf16), place[0:108])
            + dot_tn(given.first[:, layer, :].astype(bf16), place[108:162])
            + dot_tn(given.bias[layer].astype(bf16), place[162:164])
        )
        wmid[layer, block(me_w)] = given.mid[layer].astype(bf16)
        wsmall[layer, block(me_w)] = small_part.astype(bf16)

    class Spread:
        def __init__(self, weights, sems):
            self.weights, self.sems = weights, sems

        def to_chip(self, d, coming=False):
            index = 2 * (behind(chips, chip, d) if coming else chip) + core
            rows = self.weights.at[0, block(index)]
            return remote(rows, rows, self.sems, d, {WIDE: 2 * ahead(chips, chip, d) + core})

        def to_core(self, d, coming=False):
            index = 2 * behind(chips, chip, d) + (1 - core if coming else core)
            rows = self.weights.at[0, block(index)]
            return remote(rows, rows, self.sems, chips + d, {WIDE: me_w + 1 - 2 * core})

        def start(self):
            each(1, chips, lambda d: self.to_chip(d).start())
            each(0, 1, lambda d: self.to_core(d).start())

        def pass_on(self):
            def one(d):
                self.to_chip(d).wait_send()
                self.to_chip(d, True).wait_recv()
                self.to_core(d).start()

            each(1, chips, one)

        def finish(self):
            def one(d):
                self.to_core(d).wait_send()
                self.to_core(d, True).wait_recv()

            each(0, chips, one)

    spread_small, spread_mid = Spread(wsmall, at.spread[0]), Spread(wmid, at.spread[1])

    def to_all(weights, sems, layer, d):
        rows = weights.at[layer, block(me_w)]
        return remote(rows, rows, sems[layer], 0, {WIDE: ahead(wide, me_w, d)})

    later = ((wsmall, at.later[0]), (wmid, at.later[1]))

    if wide > 1:
        pl.semaphore_wait(barrier, wide * narrow - 1)
        spread_small.start()
        spread_mid.start()

    fill_masks(at.masks)
    loads.small.wait()
    to_slots = spread_rows(16, 12)
    reverse = jnp.where(slot(11 - iota((16, 12), 1)) == iota((16, 12), 0), 1.0, 0.0)
    for layer in range(layers):
        small = given.small[:, layer, :]
        lower, upper = mixing_parts(small[:, 0:12])
        scale = jnp.exp(small[:, 13:14])
        mixed = dot(reverse, dot(lower, upper, highest), highest) * as_row(scale)
        const = jnp.sum(mixed * as_row(small[:, 12:13]), axis=1, keepdims=True)
        cb = jnp.sum(to_slots * as_row(small[:, 14:15]), axis=1, keepdims=True)
        for c in range(12):
            mixes[layer, c] = jnp.broadcast_to(mixed[:, c : c + 1], (16, 128))
        mixes[layer, 12] = jnp.broadcast_to(const, (16, 128))
        mixes[layer, 13] = jnp.broadcast_to(cb, (16, 128))
        if layer:
            back = dot_nt(to_slots, mixed, highest)
            for c in range(12):
                s = c + 2 * (c // 6)
                mixes_back[layer, c] = jnp.broadcast_to(back[:, s : s + 1], (16, 128))

    def by_lanes(v):
        parts = [v[:, 128 * k : 128 * k + 128] for k in range(v.shape[1] // 128)]
        while len(parts) > 1:
            parts = [a + b for a, b in zip(parts[0::2], parts[1::2])]
        return parts[0]

    real = jnp.where(iota((8, 128), 0) < 6, 1.0, 0.0)
    first_row = jnp.where(iota((8, TILE), 0) == 0, 1.0, 0.0)

    def enter(layer, here, x):
        at.x[layer][:, here] = x
        y = wide_rows(mixes[layer, 12], TILE)
        for c in range(12):
            s = c + 2 * (c // 6)
            y = y + wide_rows(mixes[layer, c], TILE) * x[s : s + 1, :]
        taps = jnp.concatenate(shifts.taps(y[0:8]) + [first_row], axis=0)
        at.taps[layer][:, here] = taps.astype(bf16)
        at.x[layer + 1][0:8, here] = y[0:8]
        at.keep[layer][0:8, here] = y[8:16]

    def pixels_in(t, carry):
        images = TILE // 256
        blank = jnp.zeros((2, 256), f32)
        chunks = []
        for k in range(images):
            coarse = given.depth[t * images + k] == 5
            by = jnp.where(coarse, 3, 0)
            level = jnp.where(coarse, 1.0 / 32.0, 1.0 / 256.0).astype(f32)
            at_image = pl.ds(pl.multiple_of(t * TILE + k * 256, 256), 256)
            quant = lax.shift_right_logical(given.pixels[:, at_image], jnp.broadcast_to(by, (12, 256)))
            x = (quant.astype(f32) + given.noise[:, at_image]) * level - 0.5
            chunks.append(jnp.concatenate([x[0:6], blank, x[6:12], blank], axis=0))
        enter(0, tile_at(t), jnp.concatenate(chunks, axis=1))
        return carry

    tiles = count // TILE
    half = tiles // 2

    def run(first, end, body):
        lax.fori_loop(first, end, lambda t, c: (body(t), c)[1], 0)

    def piped(first, end, lead, follow):
        lead(first)

        def both(t):
            follow(t - 1)
            lead(t)

        run(first + 1, end, both)
        follow(end - 1)

    for copy in (loads.depth, loads.pixels, loads.noise, loads.prior):
        copy.wait()
    lax.fori_loop(0, tiles, pixels_in, 0)
    spread_small.pass_on()

    prior = given.prior[...]
    s = iota((55, 256), 0)
    lane = iota((55, 256), 1)
    hit = (slot(s) == lane) | (slot(s) + 72 == lane)
    to_taps = jnp.where(((s < 54) & hit) | ((s == 54) & (lane == 144)), 1.0, 0.0)
    prior_slots = dot(to_slots, prior, highest)
    parts = split_two(dot(prior_slots, to_taps, highest))
    at.prior_fwd[...] = jnp.concatenate(parts, axis=0).astype(bf16)
    turned = dot_nt(spread_rows(72, 55), prior_slots, highest)
    stacked = jnp.concatenate(split_two(turned), axis=0)
    again = jnp.where((iota((16, 32), 1) & 15) == iota((16, 32), 0), 1.0, 0.0)
    at.prior_back[...] = dot(stacked.astype(bf16), again.astype(bf16)).astype(bf16)

    whole = [group.full for group in mid + out]
    sums = [at.stat_acc, at.like_acc, at.prior_acc, at.small_acc, at.sum_acc, at.acc_in]
    for ref in whole + sums + at.bone_acc + at.acc_rest:
        ref[...] = jnp.zeros_like(ref)

    pick = jnp.where(iota((SMALL, 128), 0) == iota((SMALL, 128), 1) + OUT, 1.0, 0.0).astype(bf16)

    def derive(layer):
        w = wsmall[layer]
        win[layer] = dot(w, pick).astype(bf16)
        wst[layer] = w.T
        bone[layer] = jnp.broadcast_to(w[:, 217:218].astype(f32), (hid, 128))

    def hidden_first(layer, t):
        here = tile_at(t)
        first = dot(win[layer, :, 0:80], at.taps[layer][:, here]).astype(bf16)
        h1 = jnp.maximum(first, jnp.zeros_like(first))
        at.one[layer][:, here] = h1
        return h1

    def forward_products(layer, t):
        here = tile_at(t)
        h1 = hidden_first(layer, t) if layer else at.one[0][:, here]
        second = dot(wmid[layer], h1) + wide_rows(bone[layer], TILE)
        h2 = jnp.maximum(second, 0.0).astype(bf16)
        at.two[layer][:, here] = h2
        tbuf[...] = dot(wst[layer, 0:OUT, :], h2)

    def forward_rest(layer, t):
        here = tile_at(t)
        o = shifts.fold([tbuf[16 * k : 16 * k + 16] for k in range(9)])
        o = o + wide_rows(mixes[layer, 13], TILE)
        v = at.keep[layer][0:8, here] + o[0:8]
        decay = 1.0 + jnp.exp(-(o[8:16] + 2.0))
        q = 1.0 / decay
        at.like_acc[...] -= by_lanes(jnp.log(decay)) * real
        at.keep[layer][0:8, here] = v
        at.keep[layer][8:16, here] = q
        x = jnp.concatenate([at.x[layer + 1][0:8, here], v * q], axis=0)
        if layer < layers - 1:
            enter(layer + 1, here, x)
        else:
            at.x[layer + 1][8:16, here] = x[8:16]
            at.stat_acc[0] += by_lanes(x)
            at.stat_acc[1] += by_lanes(x * x)

    spread_small.finish()
    for layer in range(1, layers):
        for weights, sems in later:
            each(1, wide, lambda d: to_all(weights, sems, layer, d).start())
    derive(0)
    run(0, half, functools.partial(hidden_first, 0))
    spread_mid.pass_on()
    run(half, tiles, functools.partial(hidden_first, 0))
    spread_mid.finish()
    for layer in range(layers):
        if layer:
            for weights, sems in later:

                if wide > 1:
                    for sem in sems[layer]:
                        drain(weights.at[layer, 0 : (wide - 1) * share], sem)
            derive(layer)
        piped(0, tiles, functools.partial(forward_products, layer), functools.partial(forward_rest, layer))

    lane = iota((16, 128), 1)

    line = iota((16, 128), 0)
    row = jnp.where(lane == line, jnp.sum(at.stat_acc[0], axis=1, keepdims=True), 0.0)
    row = row + jnp.where(lane == line + 16, jnp.sum(at.stat_acc[1], axis=1, keepdims=True), 0.0)
    stat.start(jnp.sum(row, axis=0, keepdims=True))

    def prior_tile(t):
        here = tile_at(t)
        z1 = at.x[layers][0:8, here]
        z2 = at.x[layers][8:16, here]
        pieces = [split_two(v) for v in shifts.taps(z1)]
        tz = jnp.concatenate(
            [p[0] for p in pieces] + [p[1] for p in pieces] + [first_row, jnp.zeros_like(first_row)], axis=0
        ).astype(bf16)
        both = dot(at.prior_fwd[:, 0:160], tz)
        value = both[0:16] + both[16:32]
        centre, log_sd = value[0:8], value[8:16]
        inverse = jnp.exp(-log_sd)
        ratio = (z2 - centre) * inverse
        at.like_acc[...] += by_lanes(-0.5 * z1 * z1 - 0.5 * ratio * ratio - log_sd)
        d_centre = ratio * inverse
        d_stat = jnp.concatenate([d_centre, ratio * ratio - 1.0], axis=0)
        ds = jnp.concatenate(split_two(d_stat), axis=0).astype(bf16)
        at.prior_acc[:, 0:160] += dot_nt(ds, tz)
        dt = dot(at.prior_back[...], ds)
        dt = dt[0:72] + dt[72:144]
        folded = shifts.fold([dt[8 * k : 8 * k + 8] for k in range(9)], -1)
        gz[0:8, here] = coeff * (folded - z1)
        gz[8:16, here] = -coeff * d_centre

    run(0, tiles, prior_tile)
    for layer in range(layers):
        wmt[layer] = wmid[layer].T
    stats = stat.finish()
    mean = jnp.sum(jnp.where(lane == line, stats, 0.0), axis=1, keepdims=True) / total
    square = jnp.sum(jnp.where(lane == line + 16, stats, 0.0), axis=1, keepdims=True) / total
    var = square - mean * mean
    from_first = penalty_weight * (2.0 * mean - 4.0 * (var - 1.0) * mean) / total
    from_square = penalty_weight * 2.0 * (var - 1.0) / total
    ones_rows = jnp.where((iota((16, 1), 0) & 7) < 6, 1.0, 0.0)
    penalty = penalty_weight * jnp.sum(
        ones_rows * (mean * mean + (var - 1.0) * (var - 1.0)), axis=0, keepdims=True
    )

    def prepare_back(layer, here, g):
        v = at.keep[layer][0:8, here]
        q = at.keep[layer][8:16, here]
        gbq = g[8:16] * q
        gy_ref[0:8, here] = g[0:8]
        gy_ref[8:16, here] = gbq
        do = jnp.concatenate([gbq, (gbq * v + coeff) * (1.0 - q)], axis=0)
        at.sum_acc[layer, 1] += by_lanes(do)
        rounded = do.astype(bf16).astype(f32)
        d3[:, here] = jnp.concatenate(shifts.taps(rounded, -1), axis=0).astype(bf16)

    def last_gradient(t):
        here = tile_at(t)
        g = gz[:, here] + from_first + 2.0 * at.x[layers][:, here] * from_square
        prepare_back(layers - 1, here, g)

    def back_a(layer, t):
        here = tile_at(t)
        h2 = at.two[layer][:, here]
        taps = d3[:, here]
        grad = dot_nt(h2, taps)
        out[layer].add(grad[:, 0:128])
        at.acc_rest[layer][:, 0:16] += grad[:, 128:OUT]
        dd2 = dot(wsmall[layer, :, 0:OUT], taps).astype(bf16)
        at.two[layer][:, here] = jnp.where(h2 > 0, dd2, jnp.zeros_like(dd2))

    def back_b(layer, t):
        here = tile_at(t)
        d2 = at.two[layer][:, here]
        mid[layer].add(dot_nt(d2, at.one[layer][:, here]))
        at.bone_acc[layer][...] += by_lanes(d2.astype(f32))

    def back_c(layer, t):
        here = tile_at(t)
        dd1 = dot(wmt[layer], at.two[layer][:, here]).astype(bf16)
        h1 = at.one[layer][:, here]
        at.one[layer][:, here] = jnp.where(h1 > 0, dd1, jnp.zeros_like(dd1))

    def back_in(layer, t):
        here = tile_at(t)
        at.acc_in[:, 0:80] += dot_nt(at.one[layer][:, here], at.taps[layer][:, here])

    def back_taps(layer, t):
        tbuf[0:80] = dot(wst[layer, OUT : OUT + 80, :], at.one[layer][:, tile_at(t)])

    def back_rest(layer, t):
        here = tile_at(t)
        gya = gy_ref[0:8, here] + shifts.fold([tbuf[8 * k : 8 * k + 8] for k in range(9)], -1)
        gy = jnp.concatenate([gya, gy_ref[8:16, here]], axis=0)
        at.sum_acc[layer, 0] += by_lanes(gy)
        left = jnp.concatenate(split_two(gy), axis=0).astype(bf16)
        right = jnp.concatenate(split_two(at.x[layer][:, here]), axis=0).astype(bf16)
        at.small_acc[layer, :, 0:32] += dot_nt(left, right)
        if layer:
            gx = wide_rows(mixes_back[layer, 0], TILE) * gy[0:1, :]
            for c in range(1, 12):
                s = c + 2 * (c // 6)
                gx = gx + wide_rows(mixes_back[layer, c], TILE) * gy[s : s + 1, :]
            prepare_back(layer - 1, here, gx)

    def inner_gradient(layer):
        column = jnp.sum(at.bone_acc[layer][...], axis=1, keepdims=True)
        grad = at.acc_rest[layer][...] + pltpu.roll(at.acc_in[...], 16, 1)
        inn[layer].put(grad + jnp.where(iota((hid, 128), 1) == 217 - 128, column, 0.0))
        if layer:
            at.acc_in[...] = jnp.zeros_like(at.acc_in)

    def moments(layer):
        acc = at.small_acc[layer]
        part = acc[0:16] + acc[16:32]
        moment = jnp.where(lane < 16, part + pltpu.roll(part, 112, 1), 0.0)
        for k in range(2):
            line = jnp.sum(at.sum_acc[layer, k], axis=1, keepdims=True)
            moment = moment + jnp.where(lane == 16 + k, line, 0.0)
        return moment

    def early_sums():
        acc = at.prior_acc[0:16] + at.prior_acc[16:32]
        taps_part = (acc + pltpu.roll(acc, 256 - 72, 1))[:, 0:128]
        last = pltpu.roll(acc, 256 - 72, 1)[:, 0:128]
        pieces = [moments(layer) for layer in range(1, layers)]
        pieces.append(jnp.where(lane < 72, taps_part, 0.0) + jnp.where(lane == 72, last, 0.0))
        depths = lax.fori_loop(0, given.depth.shape[0], lambda k, c: c + given.depth[k], jnp.int32(0))
        depths = jnp.broadcast_to(depths, (8, 128)).astype(f32)
        row8 = iota((8, 128), 0)
        logs = jnp.sum(at.like_acc[...], axis=0, keepdims=True)
        pieces.append(jnp.where(row8 == 0, logs, 0.0) + jnp.where(row8 == 1, depths, 0.0))
        return jnp.concatenate(pieces, axis=0)

    def go(*which):
        for group in which:
            group.advance()

    def loop(body, layer, first=0, end=tiles):
        run(first, end, functools.partial(body, layer))

    def rest_loop(layer, first, end):
        piped(first, end, functools.partial(back_taps, layer), functools.partial(back_rest, layer))

    def inner(layer):
        inner_gradient(layer)
        inn[layer].start()

    def packed(moment):
        value = jnp.zeros((2, 128), f32)
        for k in range(6):
            pair = jnp.concatenate([moment[k : k + 1], moment[8 + k : 9 + k]], axis=0)
            value = value + (pltpu.roll(pair, 20 * k, 1) if k else pair)
        return value

    def unpacked(value):
        blank = jnp.zeros((2, 128), f32)
        turns = [pltpu.roll(value, 128 - 20 * k, 1) if k else value for k in range(6)]
        rows = [turn[0:1] for turn in turns] + [blank] + [turn[1:2] for turn in turns] + [blank]
        return jnp.where(lane < 18, jnp.concatenate(rows, axis=0), 0.0)

    run(0, tiles, last_gradient)
    loop(back_a, 1)
    out[1].start()
    loop(back_b, 1)
    mid[1].start()
    go(out[1])
    loop(back_c, 1, 0, half)
    go(mid[1])
    loop(back_c, 1, half, tiles)
    go(out[1])
    rest_loop(1, 0, tiles)
    early.start(0, early_sums())
    loop(back_a, 0)
    out[0].start()
    go(mid[1], out[1])
    early.hop()
    loop(back_b, 0)
    mid[0].start()
    go(out[0], out[1])
    loop(back_in, 1, 0, half)
    go(mid[0])
    loop(back_in, 1, half, tiles)
    inner(1)
    go(mid[1])
    early_total = early.finish(1)
    loop(back_c, 0, 0, half)
    go(inn[1], out[0])
    loop(back_c, 0, half, tiles)
    loop(back_in, 0, 0, half)
    go(mid[0], inn[1])
    loop(back_in, 0, half, tiles)
    inner(0)
    go(mid[1], out[0])
    rest_loop(0, 0, half)
    go(inn[0])
    rest_loop(0, half, tiles)
    late.start(packed(moments(0)))
    go(mid[0], inn[1], inn[0], out[0])
    go(inn[1])
    late_total = unpacked(late.finish())
    whole = jnp.concatenate([late_total, early_total], axis=0)
    rows = whole.shape[0]
    grads.sums[...] = whole + jnp.where(iota((rows, 128), 0) == rows - 8 + 2, penalty, 0.0)

    def write(group, layer, first):
        ref = group[layer].out
        grads.found[layer, :, first : first + ref.shape[1]] = ref[...]

    write(mid, 1, 0)
    write(out, 0, hid)
    write(out, 1, hid)
    write(inn, 1, hid + 128)
    go(mid[0], inn[0])
    write(mid, 0, 0)
    write(inn, 0, hid + 128)


def adamw(weight, grad, first, second, fixes):
    first_new = beta_one * first + (1.0 - beta_one) * grad
    second_new = beta_two * second + (1.0 - beta_two) * grad * grad
    update = first_new * fixes[0] / (jnp.sqrt(second_new * fixes[1]) + epsilon) + decay_rate * weight
    return (weight - learn_rate * update, first_new, second_new)


def update_kernel(total, images, step_ref, grad_ref, sums_ref, *refs):
    weights, firsts, seconds, loss_ref, outs = refs[0:6], refs[6:12], refs[12:18], refs[18], refs[19:]
    layers, share, _ = grad_ref.shape
    hid = weights[1].shape[2]
    coeff = -1.0 / (total * 12 * math.log(2.0))
    power = iota((8, 128), 1)
    used = power < jnp.broadcast_to(step_ref[0], (8, 128))
    fixes = tuple(
        1.0
        / (
            (1.0 - beta)
            * jnp.sum(
                jnp.where(used, jnp.exp(power.astype(f32) * math.log(beta)), 0.0), axis=1, keepdims=True
            )[0:1]
        )
        for beta in (beta_one, beta_two)
    )

    def write(which, at, grad):
        new = adamw(weights[which][at], grad, firsts[which][at], seconds[which][at], fixes)
        for k in range(3):
            outs[3 * which + k][at] = new[k]

    def column(layer):
        return (slice(None), layer, slice(None))

    place = spread(164, SMALL)
    to_slots = spread_rows(16, 12)
    reverse = jnp.where(slot(11 - iota((16, 12), 1)) == iota((16, 12), 0), 1.0, 0.0)
    row, col = iota((12, 12), 0), iota((12, 12), 1)
    eye = row == col
    logdet = jnp.zeros((1, 1), f32)
    for layer in range(layers):
        write(1, layer, grad_ref[layer, :, 0:hid])
        part = grad_ref[layer, :, hid : hid + SMALL]
        write(0, column(layer), dot_nt(place[108:162], part, highest))
        write(2, layer, dot_nt(part, place[0:108], highest))
        write(3, layer, dot_nt(place[162:164], part, highest))
        small = weights[4][column(layer)]
        lu = small[:, 0:12]
        lower, upper = mixing_parts(lu)
        scale = jnp.exp(small[:, 13:14])
        scale_row = as_row(scale)
        sums = sums_ref[16 * layer : 16 * layer + 16]
        turned = dot_tn(reverse, sums, highest)
        moment = dot(turned[:, 0:16], to_slots, highest)
        ones = turned[:, 16:17]
        g_mix = (moment + ones * as_row(small[:, 12:13])) * scale_row
        mix = dot(lower, upper, highest)
        g_bias = scale * dot_tn(mix, ones, highest)
        g_scale = as_column(jnp.sum(mix * g_mix, axis=0, keepdims=True)) + coeff * total
        g_lower = dot_nt(g_mix, upper, highest)
        g_upper = dot_tn(lower, g_mix, highest)
        g_lu = jnp.where(row > col, g_lower, jnp.where(eye, g_upper * jnp.exp(lu) + coeff * total, g_upper))
        g_cb = dot_tn(to_slots, sums, highest)[:, 17:18]
        wide15 = iota((12, 15), 1)
        grad = dot(g_lu, jnp.where(iota((12, 15), 0) == wide15, 1.0, 0.0), highest)
        grad = jnp.where(wide15 == 12, g_bias, grad)
        grad = jnp.where(wide15 == 13, g_scale, grad)
        grad = jnp.where(wide15 == 14, g_cb, grad)
        write(4, column(layer), grad)
        diag = jnp.sum(jnp.where(eye, lu, 0.0), axis=0, keepdims=True) + as_row(small[:, 13:14])
        logdet = logdet + jnp.sum(diag, axis=1, keepdims=True)
    sums = sums_ref[16 * layers : 16 * layers + 16]
    grad = coeff * dot_nt(
        dot_tn(to_slots, sums, highest), spread(55, 128), highest
    )
    write(5, Ellipsis, grad)
    tail = sums_ref[16 * layers + 16 :]
    likely = jnp.sum(tail[0:1], axis=1, keepdims=True)
    likely = likely - total * 6.0 * math.log(2.0 * math.pi) + total * logdet
    loss_ref[...] = coeff * likely + tail[1:2, 0:1] / images + tail[2:3, 0:1]


def turn(arrays, back=False):
    orders = ((1, 2, 0) if back else (2, 0, 1), None, (0, 2, 1), None, (1, 0, 2), None)
    return tuple(a if o is None else jnp.transpose(a, o) for a, o in zip(arrays, orders))


def shards(*args, wide, narrow):
    pixels, noise, depth, step_count = args[0:4]
    params, firsts, seconds = turn(args[4:10]), turn(args[10:16]), turn(args[16:22])
    layers, share, hid = params[1].shape
    count = pixels.shape[1]
    chips = max(wide // 2, 1)
    vmem = pltpu.VMEM

    def sems(*shape):
        return [pltpu.SemaphoreType.DMA(shape) for _ in range(2)]

    def group(across, scatter=True):
        piece = share // narrow if scatter and share % (8 * narrow) == 0 else share
        return [
            vmem((chips, hid // share // chips, share, across), f32),
            vmem((chips, share, across), f32),
            vmem((chips, share, across), f32),
            vmem((narrow, piece, across), f32),
            vmem((share, across), f32),
            [sems(1) for _ in range(4)],
        ]

    def both(height, dtype, times=layers):
        return [vmem((height, count), dtype) for _ in range(times)]

    first, middle, outer, bias, small, prior = params
    inputs = dict(
        mid=middle, first=first, out=outer, bias=bias, small=small, depth=depth, pixels=pixels, noise=noise, prior=prior
    )
    given = {
        name: pltpu.SMEM(a.shape, a.dtype) if a is depth else vmem(a.shape, a.dtype) for name, a in inputs.items()
    }
    early = 16 * layers + 8
    scratch = dict(
        given=given,
        load=pltpu.SemaphoreType.DMA((len(inputs),)),
        wmid=vmem((layers, hid, hid), bf16),
        wsmall=vmem((layers, hid, SMALL), bf16),
        wmt=vmem((layers, hid, hid), bf16),
        wst=vmem((layers, SMALL, hid), bf16),
        win=vmem((layers, hid, 128), bf16),
        bone=vmem((layers, hid, 128), f32),
        mixes=vmem((layers, 14, 16, 128), f32),
        mixes_back=vmem((layers, 12, 16, 128), f32),
        prior_fwd=vmem((32, 256), bf16),
        prior_back=vmem((144, 32), bf16),
        masks=vmem((4, 8, TILE), f32),
        gz=vmem((16, count), f32),
        gy=vmem((16, count), f32),
        d3=vmem((OUT, count), bf16),
        tbuf=vmem((OUT, TILE), f32),
        stat_acc=vmem((2, 16, 128), f32),
        like_acc=vmem((8, 128), f32),
        prior_acc=vmem((32, 256), f32),
        small_acc=vmem((layers, 32, 128), f32),
        sum_acc=vmem((layers, 2, 16, 128), f32),
        acc_in=vmem((hid, 128), f32),
        bone_acc=[vmem((hid, 128), f32) for _ in range(layers)],
        acc_rest=[vmem((hid, 128), f32) for _ in range(layers)],
        x=both(16, f32, layers + 1),
        keep=both(16, f32),
        taps=both(80, bf16),
        one=both(hid, bf16),
        two=both(hid, bf16),
        stat=[vmem((wide * narrow, 1, 128), f32), sems(1)],
        late=[vmem((wide * narrow, 2, 128), f32), sems(1)],
        early=[
            [vmem((size, early, 128), f32) for size in (wide, narrow)],
            [sems(1) for _ in range(2)],
        ],
        mid=[group(hid) for _ in range(layers)],
        out=[group(128) for _ in range(layers)],
        inn=[group(128, layer > 0) for layer in range(layers)],
        spread=[sems(2 * chips) for _ in range(2)],
        later=[[sems(1) for _ in range(layers)] for _ in range(2)],
    )
    like = jax.ShapeDtypeStruct
    grads = dict(
        found=like((layers, share, hid + SMALL), f32),
        sums=like((early + 16, 128), f32),
    )
    order = jax.tree.structure((inputs, grads, scratch))
    remote = dict(collective_id=0, has_side_effects=True) if wide > 1 else {}
    given_leaves, grad_leaves = jax.tree.leaves(inputs), jax.tree.leaves(grads)
    found = pl.pallas_call(
        functools.partial(flow_kernel, wide, narrow, order),
        out_shape=tuple(grad_leaves),
        in_specs=[HBM] * len(given_leaves),
        out_specs=(VMEM,) * len(grad_leaves),
        scratch_shapes=jax.tree.leaves(scratch),
        compiler_params=pltpu.CompilerParams(vmem_limit_bytes=FLOW_VMEM, **remote),
        name="flow",
    )(*given_leaves)
    found = SimpleNamespace(**jax.tree.unflatten(jax.tree.structure(grads), found))
    total = count * wide * narrow
    shapes = [like((1, 1), f32)] + [like(p.shape, f32) for p in params for _ in range(3)]
    results = pl.pallas_call(
        functools.partial(update_kernel, total, total // 256),
        out_shape=tuple(shapes),
        in_specs=[SMEM] + [VMEM] * 20,
        out_specs=(VMEM,) * 19,
        compiler_params=pltpu.CompilerParams(vmem_limit_bytes=UPDATE_VMEM),
        name="update",
    )(step_count.reshape(1), found.found, found.sums, *params, *firsts, *seconds)
    updated = [turn(results[1 + k :: 3], True) for k in range(3)]
    return (results[0].reshape(()),) + tuple(updated[k][p] for p in range(6) for k in range(3))


def solution(mesh):
    pixels = P(None, (NARROW, WIDE))
    rows, columns = P(None, WIDE, None), P(None, None, WIDE)
    weights = (rows, rows, columns, columns, P(), P())
    return jax.shard_map(
        functools.partial(shards, wide=mesh.shape[WIDE], narrow=mesh.shape[NARROW]),
        mesh=mesh,
        in_specs=(pixels, pixels, P((NARROW, WIDE)), P()) + weights * 3,
        out_specs=(P(),) + tuple(w for w in weights for _ in range(3)),
        check_vma=False,
    )
```

time: 114 us -> 101 us (0.89)
  Pallas kernels: 112 us -> 99.8 us
    pallas_call x1, Pallas kernels: 108 us -> 95.7 us  [shards(): pl.pallas_call(functools.partial(flow_kernel, wide, narrow, order), out_s...]
where the time goes in v3:
time: 101 us
  Pallas kernels  99.8 us (99%)
  between operations  1.49 us (1%)
    pallas_call x1, Pallas kernels, shards(): pl.pallas_call(functools.partial(flow_kernel, wide, narrow, order), out_s...  95.7 us
    pallas_call x1, Pallas kernels, shards(): pl.pallas_call(functools.partial(update_kernel, total, total // 256), out...  4.09 us

profile of v3, /device:TPU:0, one launch (start us, length us, event | category | flops | bytes accessed | tf_op | source)
XLA Modules:
  0.0 101.2 jit_solution(2916970401247207402)
XLA Ops:
  1.3 95.7 %flow.1 = (f32[2,64,768]{2,1,0:T(8,128)}, f32[56,128]{1,0:T(8,128)}) custom-call(f32[2,2,64]{2,1,0:T(2,128)} %refs_3_.3, s32[32]{0:T(128)} %refs_1_.2, f32[54,2,64]{2,1,0:T(2,128)} %bitcast.23, f32[2,64,512]{2,1,0:T(8,128)} %refs_1_.3, f32[12,8192]{1,0:T(8,128)} %refs_4_.1, f32[2,64,108]{2,1,0:T(8,128)} %bitcast.21, s32[12,8192]{1,0:T(8,128)} %refs_6_.1, ...), custom_call_target="tpu_custom_call" | custom-call | tf_op jit(solution)/shard_map/flow/pallas_call | solution.py:946
  97.0 4.1 %update.1 = (f32[1,1]{1,0:T(1,128)}, f32[54,2,64]{2,1,0:T(2,128)}, f32[54,2,64]{2,1,0:T(2,128)}, f32[54,2,64]{2,1,0:T(2,128)}, f32[2,64,512]{2,1,0:T(8,128)}, /*...) custom-call(s32[1]{0:T(128)} %bitcast.20.step_ref, ...), custom_call_target="tpu_custom_call" | custom-call | tf_op jit(solution)/shard_map/update/pallas_call | solution.py:958

commit v4 on v3

--- a/solution.py
+++ b/solution.py
@@ -716,41 +716,45 @@
         rows = [turn[0:1] for turn in turns] + [blank] + [turn[1:2] for turn in turns] + [blank]
         return jnp.where(lane < 18, jnp.concatenate(rows, axis=0), 0.0)
 
-    run(0, tiles, last_gradient)
-    loop(back_a, 1)
+    piped(0, tiles, last_gradient, functools.partial(back_a, 1))
     out[1].start()
-    loop(back_b, 1)
+    def lead(t):
+        back_b(1, t)
+        back_c(1, t)
+
+    def follow(t):
+        back_taps(1, t)
+        back_rest(1, t)
+
+    piped(0, tiles, lead, follow)
     mid[1].start()
     go(out[1])
-    loop(back_c, 1, 0, half)
+    early.start(0, early_sums())
+    loop(back_a, 0, 0, half)
     go(mid[1])
-    loop(back_c, 1, half, tiles)
+    loop(back_a, 0, half, tiles)
+    out[0].start()
     go(out[1])
-    rest_loop(1, 0, tiles)
-    early.start(0, early_sums())
-    loop(back_a, 0)
-    out[0].start()
-    go(mid[1], out[1])
     early.hop()
     loop(back_b, 0)
     mid[0].start()
-    go(out[0], out[1])
+    go(mid[1], out[0], out[1])
     loop(back_in, 1, 0, half)
     go(mid[0])
     loop(back_in, 1, half, tiles)
     inner(1)
-    go(mid[1])
     early_total = early.finish(1)
     loop(back_c, 0, 0, half)
-    go(inn[1], out[0])
+    go(inn[1], out[0], out[1])
     loop(back_c, 0, half, tiles)
+    go(mid[1])
     loop(back_in, 0, 0, half)
     go(mid[0], inn[1])
     loop(back_in, 0, half, tiles)
     inner(0)
-    go(mid[1], out[0])
+    go(out[0])
     rest_loop(0, 0, half)
-    go(inn[0])
+    go(inn[0], mid[1])
     rest_loop(0, half, tiles)
     late.start(packed(moments(0)))
     go(mid[0], inn[1], inn[0], out[0])

time: 101 us -> 99.6 us (0.986)
  Pallas kernels: 99.8 us -> 97.9 us
    pallas_call x1, Pallas kernels: 95.7 us -> 93.8 us  [shards(): pl.pallas_call(functools.partial(flow_kernel, wide, narrow, order), out_s...]
where the time goes in v4:
time: 99.6 us; the launch traced here: 99.4 us
  Pallas kernels  97.9 us (98%)
  between operations  1.49 us (1%)
    pallas_call x1, Pallas kernels, shards(): pl.pallas_call(functools.partial(flow_kernel, wide, narrow, order), out_s...  93.8 us
    pallas_call x1, Pallas kernels, shards(): pl.pallas_call(functools.partial(update_kernel, total, total // 256), out...  4.09 us

profile of v4, /device:TPU:0, one launch (start us, length us, event | category | flops | bytes accessed | tf_op | source)
XLA Modules:
  0.0 99.4 jit_solution(3101962174083786712)
XLA Ops:
  1.3 93.8 %flow.1 = (f32[2,64,768]{2,1,0:T(8,128)}, f32[56,128]{1,0:T(8,128)}) custom-call(f32[2,2,64]{2,1,0:T(2,128)} %refs_3_.3, s32[32]{0:T(128)} %refs_1_.2, f32[54,2,64]{2,1,0:T(2,128)} %bitcast.23, f32[2,64,512]{2,1,0:T(8,128)} %refs_1_.3, f32[12,8192]{1,0:T(8,128)} %refs_4_.1, f32[2,64,108]{2,1,0:T(8,128)} %bitcast.21, s32[12,8192]{1,0:T(8,128)} %refs_6_.1, ...), custom_call_target="tpu_custom_call" | custom-call | tf_op jit(solution)/shard_map/flow/pallas_call | solution.py:950
  95.1 4.1 %update.1 = (f32[1,1]{1,0:T(1,128)}, f32[54,2,64]{2,1,0:T(2,128)}, f32[54,2,64]{2,1,0:T(2,128)}, f32[54,2,64]{2,1,0:T(2,128)}, f32[2,64,512]{2,1,0:T(8,128)}, /*...) custom-call(s32[1]{0:T(128)} %bitcast.20.step_ref, ...), custom_call_target="tpu_custom_call" | custom-call | tf_op jit(solution)/shard_map/update/pallas_call | solution.py:962

commit v5 on v4

--- a/solution.py
+++ b/solution.py
@@ -328,8 +328,8 @@
                 barrier,
                 inc=1,
                 device_id={
-                    NARROW: ahead(narrow, me_n, d // wide),
-                    WIDE: ahead(wide, me_w, lax.rem(d, wide)),
+                    NARROW: behind(narrow, me_n, (wide * narrow - d) // wide),
+                    WIDE: behind(wide, me_w, lax.rem(wide * narrow - d, wide)),
                 },
                 device_id_type=MESH,
             ),
@@ -523,9 +523,10 @@
         o = shifts.fold([tbuf[16 * k : 16 * k + 16] for k in range(9)])
         o = o + wide_rows(mixes[layer, 13], TILE)
         v = at.keep[layer][0:8, here] + o[0:8]
-        decay = 1.0 + jnp.exp(-(o[8:16] + 2.0))
-        q = 1.0 / decay
-        at.like_acc[...] -= by_lanes(jnp.log(decay)) * real
+        u = o[8:16] + 2.0
+        decay = jnp.exp(-jnp.abs(u))
+        q = jnp.where(u >= 0.0, 1.0, decay) / (1.0 + decay)
+        at.like_acc[...] += by_lanes(jnp.minimum(u, 0.0) - jnp.log(1.0 + decay)) * real
         at.keep[layer][0:8, here] = v
         at.keep[layer][8:16, here] = q
         x = jnp.concatenate([at.x[layer + 1][0:8, here], v * q], axis=0)

time: 99.6 us -> 99.6 us (level)
  no operation moved by 1% of the time
where the time goes in v5:
time: 99.6 us; the launch traced here: 99.4 us
  Pallas kernels  97.9 us (98%)
  between operations  1.49 us (1%)
    pallas_call x1, Pallas kernels, shards(): pl.pallas_call(functools.partial(flow_kernel, wide, narrow, order), out_s...  93.8 us
    pallas_call x1, Pallas kernels, shards(): pl.pallas_call(functools.partial(update_kernel, total, total // 256), out...  4.09 us

profile of v5, /device:TPU:0, one launch (start us, length us, event | category | flops | bytes accessed | tf_op | source)
XLA Modules:
  0.0 99.4 jit_solution(3025174417525642733)
XLA Ops:
  1.3 93.8 %flow.1 = (f32[2,64,768]{2,1,0:T(8,128)}, f32[56,128]{1,0:T(8,128)}) custom-call(f32[2,2,64]{2,1,0:T(2,128)} %refs_3_.3, s32[32]{0:T(128)} %refs_1_.2, f32[54,2,64]{2,1,0:T(2,128)} %bitcast.23, f32[2,64,512]{2,1,0:T(8,128)} %refs_1_.3, f32[12,8192]{1,0:T(8,128)} %refs_4_.1, f32[2,64,108]{2,1,0:T(8,128)} %bitcast.21, s32[12,8192]{1,0:T(8,128)} %refs_6_.1, ...), custom_call_target="tpu_custom_call" | custom-call | tf_op jit(solution)/shard_map/flow/pallas_call | solution.py:951
  95.1 4.1 %update.1 = (f32[1,1]{1,0:T(1,128)}, f32[54,2,64]{2,1,0:T(2,128)}, f32[54,2,64]{2,1,0:T(2,128)}, f32[54,2,64]{2,1,0:T(2,128)}, f32[2,64,512]{2,1,0:T(8,128)}, /*...) custom-call(s32[1]{0:T(128)} %bitcast.20.step_ref, ...), custom_call_target="tpu_custom_call" | custom-call | tf_op jit(solution)/shard_map/update/pallas_call | solution.py:963
